TPU v7x, 128 devices: a whole 4x4x4 slice. The times are simulated.
128 devices in a mesh: shot: 4 (over z_lo, core), space: 32 (over y, z_hi, x).
Axes of the slice: x: 4, y: 4, z: 4 (z_hi: 2, z_lo: 2; z = z_hi * 2 + z_lo), core: 2. Of those that a mesh axis runs over, the one named last changes fastest.
Arguments:
- adjoint_state: float32 [4, 9, 512, 64, 128], P('shot', None, 'space'), may hold values from -6 to 6
- forward_velocity: float32 [4, 4, 3, 512, 64, 128], P('shot', None, None, 'space'), may hold values from -6 to 6
- vp: float32 [512, 64, 128], P('space'), may hold values from 1 to 1.8
- shear_ratio: float32 [512, 64, 128], P('space'), may hold values from 0.45 to 0.65
- density: float32 [512, 64, 128], P('space'), may hold values from 1 to 2.5
- residuals: float32 [4, 3, 32768], P('shot', None, 'space'), may hold values from -12 to 12
- owner: int32 [32768, 1], P('space'), may hold values from 0 to 31; in each aligned block of 1024 rows (0 to 1023, 1024 to 2047, ...) at most 128 rows name the same one
- cell: int32 [32768], P('space'), may hold values from 0 to 131071
Outputs:
- adjoint_final: float32 [4, 9, 512, 64, 128], P('shot', None, 'space')
- gradient: float32 [3, 512, 64, 128], P(None, 'space', 'shot')
Inputs may be any that keep to these rules, and one draw needn't show every extreme that they name: Among the 1024 channels of one device no owner appears more than 128 times, and some owner appears exactly 128 times.
All inputs are finite; a program needn't handle non-finite values.
Results may differ from a plain program's by a relative error of at most 0.000032.
Values sent between devices are 32-bit elements; how exact they have to be, the bound alone decides.
A program may use at most 128 MiB of HBM per device.

v0:
```python
import jax
import jax.numpy as jnp
from jax import lax
from jax.sharding import PartitionSpec as P

CAP = 128
STEPS = 3
SWEEPS = 2


COURANT = 0.3
KAPPA = 0.15


def with_halo(cells, sides, width):
    for axis, dim in sides:
        count = lax.axis_size(axis)
        ends = count - 1
        head = lax.slice_in_dim(cells, 0, width, axis=dim)
        tail = lax.slice_in_dim(cells, cells.shape[dim] - width, cells.shape[dim], axis=dim)
        cells = jnp.concatenate(
            [
                lax.ppermute(tail, axis, [(i, (i + 1) % count) for i in range(ends)]),
                cells,
                lax.ppermute(head, axis, [((i + 1) % count, i) for i in range(ends)]),
            ],
            axis=dim,
        )
    return cells


def plus(f, axis):
    widths = [(0, 0)] * f.ndim
    widths[axis] = (0, 1)
    padded = jnp.pad(f, widths)
    return lax.slice_in_dim(padded, 1, f.shape[axis] + 1, axis=axis) - f


def minus(f, axis):
    widths = [(0, 0)] * f.ndim
    widths[axis] = (1, 0)
    padded = jnp.pad(f, widths)
    return f - lax.slice_in_dim(padded, 0, f.shape[axis], axis=axis)


def xplus(padded):
    return padded[2:] - padded[1:-1]


def xminus(padded):
    return padded[1:-1] - padded[:-2]


def advance(fields, buoy, lam, shear):
    vx, vy, vz, sxx, syy, szz, sxy, sxz, syz = fields
    stress_rim = with_halo(jnp.stack([sxx, sxy, sxz]), (("space", 1),), 1)
    dxx = xplus(stress_rim[0])
    dxy = xminus(stress_rim[1])
    dxz = xminus(stress_rim[2])
    vx = vx + COURANT * buoy * (dxx + minus(sxy, 1) + minus(sxz, 2))
    vy = vy + COURANT * buoy * (dxy + plus(syy, 1) + minus(syz, 2))
    vz = vz + COURANT * buoy * (dxz + minus(syz, 1) + plus(szz, 2))
    speed_rim = with_halo(jnp.stack([vx, vy, vz]), (("space", 1),), 1)
    exx = xminus(speed_rim[0])
    pvy = xplus(speed_rim[1])
    pvz = xplus(speed_rim[2])
    eyy = minus(vy, 1)
    ezz = minus(vz, 2)
    div = exx + eyy + ezz
    sxx = sxx + COURANT * (lam * div + 2.0 * shear * exx)
    syy = syy + COURANT * (lam * div + 2.0 * shear * eyy)
    szz = szz + COURANT * (lam * div + 2.0 * shear * ezz)
    sxy = sxy + COURANT * shear * (pvy + plus(vx, 1))
    sxz = sxz + COURANT * shear * (pvz + plus(vx, 2))
    syz = syz + COURANT * shear * (plus(vz, 1) + plus(vy, 2))
    return [vx, vy, vz, sxx, syy, szz, sxy, sxz, syz]


def local(adjoint_state, forward_velocity, vp, shear_ratio, density, residuals, owner, cell):
    buoy = 1.0 / density
    speed_s = shear_ratio * vp
    shear = density * speed_s * speed_s
    lam = density * vp * vp - 2.0 * shear
    width_x, width_y, width_z = vp.shape
    n_space = lax.axis_size("space")
    owners = owner[:, 0]
    onehot = (owners[:, None] == jnp.arange(n_space, dtype=jnp.int32)[None, :]).astype(jnp.int32)
    ranks = jnp.cumsum(onehot, axis=0) - 1
    slots = jnp.sum(ranks * onehot, axis=1)
    payload = jnp.concatenate([residuals[0].T, cell[:, None].astype(jnp.float32)], axis=1)
    packed = jnp.zeros((n_space, STEPS + 1, CAP), jnp.float32).at[owners, :, slots].set(payload)
    arrived = lax.all_to_all(packed, "space", split_axis=0, concat_axis=0, tiled=True)
    targets = arrived[:, STEPS, :].reshape(-1).astype(jnp.int32)
    fwd = forward_velocity[0]
    fwd_rim = with_halo(
        fwd[:STEPS].reshape(STEPS * 3, width_x, width_y, width_z), (("space", 1),), 1
    )
    fwd_rim = fwd_rim.reshape(STEPS, 3, width_x + 2, width_y, width_z)
    fwd_dxx = [xminus(fwd_rim[t, 0]) for t in range(STEPS)]
    fwd_pyx = [xplus(fwd_rim[t, 1]) for t in range(STEPS)]
    fwd_pzx = [xplus(fwd_rim[t, 2]) for t in range(STEPS)]
    fields = [adjoint_state[0, k] for k in range(9)]
    glam = jnp.zeros(vp.shape, jnp.float32)
    gmu = jnp.zeros(vp.shape, jnp.float32)
    grho = jnp.zeros(vp.shape, jnp.float32)
    for step in range(STEPS):
        fields = advance(fields, buoy, lam, shear)
        szz_flat = fields[5].reshape(-1).at[targets].add(arrived[:, step, :].reshape(-1))
        fields[5] = szz_flat.reshape(vp.shape)
        ux, uy, uz = (fwd[step, 0], fwd[step, 1], fwd[step, 2])
        wx, wy, wz = (fwd[step + 1, 0], fwd[step + 1, 1], fwd[step + 1, 2])
        vx, vy, vz, sxx, syy, szz, sxy, sxz, syz = fields
        fxx = fwd_dxx[step]
        fyy = minus(uy, 1)
        fzz = minus(uz, 2)
        glam = glam + (fxx + fyy + fzz) * (sxx + syy + szz)
        gmu = (
            gmu
            + 2.0 * (fxx * sxx + fyy * syy + fzz * szz)
            + (fwd_pyx[step] + plus(ux, 1)) * sxy
            + (fwd_pzx[step] + plus(ux, 2)) * sxz
            + (plus(uz, 1) + plus(uy, 2)) * syz
        )
        grho = grho + vx * (wx - ux) + vy * (wy - uy) + vz * (wz - uz)
    terms = jnp.stack([glam, gmu, grho])
    share_y = width_y // lax.axis_size("shot")
    grad = lax.psum(terms, "shot")
    for sweep in range(SWEEPS):
        rim = with_halo(grad, (("space", 1),), 1)
        inner = jnp.pad(grad, ((0, 0), (0, 0), (1, 1), (1, 1)))
        near = rim[:, 2:] + rim[:, :-2]
        near = near + inner[:, :, 2:, 1:-1] + inner[:, :, :-2, 1:-1]
        near = near + inner[:, :, 1:-1, 2:] + inner[:, :, 1:-1, :-2]
        grad = grad + KAPPA * (near - 6.0 * grad)
    grad = lax.dynamic_slice_in_dim(grad, lax.axis_index("shot") * share_y, share_y, 2)
    return (jnp.stack(fields)[None], grad)


def solution(mesh):
    in_specs = (
        P("shot", None, "space", None, None),
        P("shot", None, None, "space", None, None),
        P("space", None, None),
        P("space", None, None),
        P("space", None, None),
        P("shot", None, "space"),
        P("space", None),
        P("space"),
    )
    out_specs = (P("shot", None, "space", None, None), P(None, "space", "shot", None))
    return jax.shard_map(local, mesh=mesh, in_specs=in_specs, out_specs=out_specs, check_vma=False)
```

profile of v0, /device:TPU:9, one launch (start us, length us, event | category | flops | bytes accessed | tf_op | source)
XLA Modules:
  0.0 346.1 jit_solution(6532934542019581254)
XLA Ops:
  7.2 3.6 %slice_bitcast_fusion.15 = (f32[16,64,128]{2,1,0:T(8,128)}, f32[16,64,128]{2,1,0:T(8,128)}, f32[16,64,128]{2,1,0:T(8,128)S(1)}, f32[16,64,128]{2,1,0:T(8,128)}, ...) fusion(f32[1,9,16,64,128]{4,3,2,1,0:T(8,128)} %param.8), kind=kLoop, calls=%fused_computation.369 | loop fusion | bytes 7340032 | tf_op jit(solution)/shard_map/squeeze | solution.py:102
  10.8 3.3 collective-permute-start.1
  14.1 6.7 %collective-permute-start = (f32[3,1,64,128]{3,2,1,0:T(8,128)S(1)}, f32[3,1,64,128]{3,2,1,0:T(8,128)}, u32[]{:S(2)}, u32[]{:S(2)}) collective-permute-start(f32[3,1,64,128]{3,2,1,0:T(8,128)S(1)} %get-tuple-element.69), channel_id=1, source_target_pairs={{1,0},{2,1},{3,2},{4,3},{5,4},{6,5},{7,6},{8,7},{9,8},{10,9},{11,1... | collective-permute-start | bytes 294920 | tf_op jit(solution)/shard_map/ppermute | solution.py:25
  20.8 9.0 %reduce-window.6 = s32[32,8,128]{2,1,0:T(8,128)S(1)} reduce-window(s32[32,8,128]{2,1,0:T(8,128)S(1)} %fusion.215, s32[]{:T(128)} %constant.8.clone.1), window={size=1x1x128 pad=0_0x0_0x127_0}, to_apply=%region_0.0 | reduce-window | flops 4161536 | bytes 262148 | tf_op jit(solution)/shard_map/reduce-window
  30.8 4.5 %scatter_custom_fusion.3 = f32[4096,4]{1,0:T(8,128)} fusion(s32[1024]{0:T(1024)S(1)} %broadcast_select_fusion, f32[1024,4]{1,0:T(8,128)S(1)} %copy.20, f32[]{:T(128)} %constant.17.clone.1), kind=kCustom, calls=%fused_computation.27 | custom fusion | bytes 65540
  35.3 2.8 copy.21
  38.2 6.9 %all-to-all-start = ((f32[32,4,128]{2,1,0:T(4,128)}), f32[32,4,128]{2,1,0:T(4,128)S(1)}, u32[]{:S(2)}, u32[]{:S(2)}) async-start(f32[32,4,128]{2,1,0:T(4,128)} %bitcast.38), calls=%async_computation | async-start | bytes 131072 | tf_op jit(solution)/shard_map/all_to_all | solution.py:92
  45.2 1.9 fusion.21
  47.2 2.0 fusion.26
  49.2 1.7 fusion.16
  51.0 3.1 collective-permute-start.2
  54.8 6.7 %collective-permute-start.3 = (f32[3,1,64,128]{3,2,1,0:T(8,128)S(1)}, f32[3,1,64,128]{3,2,1,0:T(8,128)S(1)}, u32[]{:S(2)}, u32[]{:S(2)}) collective-permute-start(f32[3,1,64,128]{3,2,1,0:T(8,128)S(1)} %get-tuple-element.67), channel_id=1, source_target_pairs={{1,0},{2,1},{3,2},{4,3},{5,4},{6,5},{7,6},{8,7},{9,8},{10,9},{11,1... | collective-permute-start | bytes 294920 | tf_op jit(solution)/shard_map/ppermute | solution.py:25
  61.5 1.9 multiply_add_fusion.6
  63.5 2.7 multiply_add_fusion.7
  66.1 2.9 fusion.31
  69.1 5.2 %collective-permute-start.4 = (f32[3,1,64,128]{3,2,1,0:T(8,128)S(1)}, f32[3,1,64,128]{3,2,1,0:T(8,128)S(1)}, u32[]{:S(2)}, u32[]{:S(2)}) collective-permute-start(f32[3,1,64,128]{3,2,1,0:T(8,128)S(1)} %get-tuple-element.65), channel_id=1, source_target_pairs={{1,0},{2,1},{3,2},{4,3},{5,4},{6,5},{7,6},{8,7},{9,8},{10,9},{11,1... | collective-permute-start | bytes 294920 | tf_op jit(solution)/shard_map/ppermute | solution.py:25
  74.3 1.9 collective-permute-start.5
  76.3 26.3 %scatter_fusion = f32[131072]{0:T(1024)S(1)} fusion(f32[131072]{0:T(1024)S(1)} %bitcast.351, s32[4096]{0:T(1024)S(1)} %bitcast.418, f32[4096]{0:T(1024)} %bitcast.423), kind=kCustom, calls=%fused_computation | custom fusion | flops 4096 | bytes 65536 | tf_op jit(solution)/shard_map/scatter-add | solution.py:108
  102.7 2.0 fusion.36
  105.6 4.5 %collective-permute-start.7 = (f32[3,1,64,128]{3,2,1,0:T(8,128)S(1)}, f32[3,1,64,128]{3,2,1,0:T(8,128)S(1)}, u32[]{:S(2)}, u32[]{:S(2)}) collective-permute-start(f32[3,1,64,128]{3,2,1,0:T(8,128)S(1)} %get-tuple-element.63), channel_id=1, source_target_pairs={{1,0},{2,1},{3,2},{4,3},{5,4},{6,5},{7,6},{8,7},{9,8},{10,9},{11,1... | collective-permute-start | bytes 294920 | tf_op jit(solution)/shard_map/ppermute | solution.py:25
  110.1 2.2 collective-permute-start.6
  112.3 3.1 fusion.226
  115.5 4.6 %collective-permute-done.6 = f32[3,1,64,128]{3,2,1,0:T(8,128)S(1)} collective-permute-done((f32[3,1,64,128]{3,2,1,0:T(8,128)S(1)}, f32[3,1,64,128]{3,2,1,0:T(8,128)S(1)}, u32[]{:S(2)}, u32[]{:S(2)}) %collective-permute-start.6) | collective-permute-done | bytes 98336 | tf_op jit(solution)/shard_map/ppermute | solution.py:23
  120.8 1.7 multiply_add_fusion.4
  124.0 3.3 collective-permute-start.8
  127.3 2.0 collective-permute-start.9
  130.2 1.9 collective-permute-start.12
  132.1 7.9 %collective-permute-start.13 = (f32[9,1,64,128]{3,2,0,1:T(8,128)}, f32[9,1,64,128]{3,2,0,1:T(8,128)}, u32[]{:S(2)}, u32[]{:S(2)}) collective-permute-start(f32[9,1,64,128]{3,2,0,1:T(8,128)} %get-tuple-element.37), channel_id=1, source_target_pairs={{1,0},{2,1},{3,2},{4,3},{5,4},{6,5},{7,6},{8,7},{9,8},{10,9},{11,1... | collective-permute-start | bytes 884744 | tf_op jit(solution)/shard_map/ppermute | solution.py:25
  140.0 26.3 %scatter_fusion.1 = f32[131072]{0:T(1024)S(1)} fusion(f32[131072]{0:T(1024)S(1)} %bitcast.346, s32[4096]{0:T(1024)S(1)} %bitcast.419, f32[4096]{0:T(1024)} %bitcast.422), kind=kCustom, calls=%fused_computation.1 | custom fusion | flops 4096 | bytes 65536 | tf_op jit(solution)/shard_map/scatter-add | solution.py:108
  166.4 8.4 %fusion.163 = (f32[1,16,64,128]{3,2,1,0:T(8,128)}, f32[16,64,128]{2,1,0:T(8,128)S(1)}, f32[16,64,128]{2,1,0:T(8,128)S(1)}, f32[16,64,128]{2,1,0:T(8,128)S(1)}) fusion(f32[4,3,16,64,128]{4,3,2,1,0:T(8,128)} %bitcast.380, f32[16,64,128]{2,1,0:T(8,128)} %copy-done.16, f32[16,64,128]{2,1,0:T(8,128)} %copy-done.21, f32[16,64,128]{2,1,0:T(8,128)} %copy-done.20, ...), kind=kLoop, calls=%fused_computation.237 | loop fusion | flops 7602176 | bytes 16973824 | tf_op jit(solution)/shard_map/stack | solution.py:125
  174.9 2.1 collective-permute-start.10
  177.0 2.2 slice_bitcast_fusion.3
  179.2 7.9 %collective-permute-start.11 = (f32[3,1,64,128]{3,2,1,0:T(8,128)S(1)}, f32[3,1,64,128]{3,2,1,0:T(8,128)}, u32[]{:S(2)}, u32[]{:S(2)}) collective-permute-start(f32[3,1,64,128]{3,2,1,0:T(8,128)S(1)} %get-tuple-element.58), channel_id=1, source_target_pairs={{1,0},{2,1},{3,2},{4,3},{5,4},{6,5},{7,6},{8,7},{9,8},{10,9},{11,1... | collective-permute-start | bytes 294920 | tf_op jit(solution)/shard_map/ppermute | solution.py:25
  187.1 3.1 multiply_add_fusion
  190.2 26.6 %scatter_fusion.2 = f32[131072]{0:T(1024)S(1)} fusion(f32[131072]{0:T(1024)S(1)} %bitcast.356, s32[4096]{0:T(1024)S(1)} %bitcast.420, f32[4096]{0:T(1024)} %bitcast.421), kind=kCustom, calls=%fused_computation.2 | custom fusion | flops 4096 | bytes 65536 | tf_op jit(solution)/shard_map/scatter-add | solution.py:108
  216.9 8.3 %add_bitcast_fusion = (f32[1,16,64,128]{3,2,1,0:T(8,128)}, f32[16,64,128]{2,1,0:T(8,128)}, f32[16,64,128]{2,1,0:T(8,128)}) fusion(f32[16,64,128]{2,1,0:T(8,128)S(1)} %bitcast.357, f32[16,64,128]{2,1,0:T(8,128)S(1)} %bitcast.349, f32[16,64,128]{2,1,0:T(8,128)} %copy-done.25, f32[16,64,128]{2,1,0:T(8,128)} %get-tuple-element.48, ...), kind=kLoop, calls=%fused_computation.353 | loop fusion | flops 6291456 | bytes 17596416 | tf_op jit(solution)/shard_map/stack | solution.py:125
  226.0 10.6 %fusion.101 = (f32[1,16,64,128]{3,2,1,0:T(8,128)}, f32[16,64,128]{2,1,0:T(8,128)}, f32[16,64,128]{2,1,0:T(8,128)}, f32[16,64,128]{2,1,0:T(8,128)}) fusion(f32[16,64,128]{2,1,0:T(8,128)S(1)} %copy-done.2, f32[16,64,128]{2,1,0:T(8,128)} %get-tuple-element.28, f32[16,64,128]{2,1,0:T(8,128)S(1)} %copy-done.35, f32[16,64,128]{2,1,0:T(8,128)} %get-tuple-element.33, ...), kind=kLoop, calls=%fused_computation.174 | loop fusion | flops 13762560 | bytes 28475392 | tf_op jit(solution)/shard_map/stack | solution.py:125
  236.6 2.7 pad_maximum_fusion.4
  245.5 55.3 %all-reduce.58.cloned.1.call-done = f32[3,16,64,128]{3,2,1,0:T(8,128)} async-done(((f32[3,16,64,128]{3,2,1,0:T(8,128)}), f32[3,16,64,128]{3,2,1,0:T(8,128)}) %all-reduce.58.cloned.1.call-update) | async-done | bytes 1572880 | tf_op jit(solution)/shard_map/psum | solution.py:127
  301.8 6.6 %collective-permute-start.14 = (f32[3,1,64,128]{3,2,1,0:T(8,128)S(1)}, f32[3,1,64,128]{3,2,1,0:T(8,128)S(1)}, u32[]{:S(2)}, u32[]{:S(2)}) collective-permute-start(f32[3,1,64,128]{3,2,1,0:T(8,128)S(1)} %get-tuple-element.56), channel_id=1, source_target_pairs={{1,0},{2,1},{3,2},{4,3},{5,4},{6,5},{7,6},{8,7},{9,8},{10,9},{11,1... | collective-permute-start | bytes 294920 | tf_op jit(solution)/shard_map/ppermute | solution.py:25
  308.4 1.9 collective-permute-start.15
  311.2 7.4 %collective-permute-done.15 = f32[3,1,64,128]{3,2,1,0:T(8,128)S(1)} collective-permute-done((f32[3,1,64,128]{3,2,1,0:T(8,128)S(1)}, f32[3,1,64,128]{3,2,1,0:T(8,128)S(1)}, u32[]{:S(2)}, u32[]{:S(2)}) %collective-permute-start.15) | collective-permute-done | bytes 98336 | tf_op jit(solution)/shard_map/ppermute | solution.py:23
  318.6 6.5 %fusion.6 = f32[3,16,64,128]{3,2,1,0:T(8,128)S(1)} fusion(f32[3,16,64,128]{3,2,1,0:T(8,128)} %all-reduce.58.cloned.1.call-done, f32[3,1,64,128]{3,2,1,0:T(8,128)S(1)} %collective-permute-done.15, f32[3,1,64,128]{3,2,1,0:T(8,128)S(1)} %collective-permute-done.14), kind=kLoop, calls=%fused_computation.18 | loop fusion | flops 4325376 | bytes 3342336 | tf_op jit(solution)/shard_map/add | solution.py:134
  325.1 1.9 collective-permute-start.16
  327.0 3.4 collective-permute-start.17
  331.2 5.7 %collective-permute-done.17 = f32[3,1,64,128]{3,2,1,0:T(8,128)S(1)} collective-permute-done((f32[3,1,64,128]{3,2,1,0:T(8,128)S(1)}, f32[3,1,64,128]{3,2,1,0:T(8,128)S(1)}, u32[]{:S(2)}, u32[]{:S(2)}) %collective-permute-start.17) | collective-permute-done | bytes 98336 | tf_op jit(solution)/shard_map/ppermute | solution.py:23
  336.9 1.4 fusion.7
  338.3 1.0 fusion.212
  (180 shorter events, 15.2 us)
Async XLA Ops:
  7.2 13.6 %copy-start.48 = (s32[1024,1]{0,1:T(1,128)S(1)}, s32[1024,1]{0,1:T(1,128)}, u32[]{:S(2)}) copy-start(s32[1024,1]{0,1:T(1,128)} %param.14) | copy-start | bytes 12292
  10.8 34.4 %copy-start.37 = (f32[16,64,128]{2,1,0:T(8,128)}, f32[16,64,128]{2,1,0:T(8,128)S(1)}, u32[]{:S(2)}) copy-start(f32[16,64,128]{2,1,0:T(8,128)S(1)} %get-tuple-element.41) | copy-start | bytes 1572868
  10.8 36.4 %copy-start.27 = (f32[1,16,64,128]{3,2,1,0:T(8,128)}, f32[1,16,64,128]{3,2,1,0:T(8,128)S(1)}, u32[]{:S(2)}) copy-start(f32[1,16,64,128]{3,2,1,0:T(8,128)S(1)} %get-tuple-element.45) | copy-start | bytes 1572868
  10.8 19.6 %copy-start.52 = (s32[2]{0:T(128)S(1)}, s32[2]{0:T(128)}, u32[]{:S(2)}) copy-start(s32[2]{0:T(128)} %constant.158) | copy-start | bytes 28
  10.8 19.7 %copy-start.51 = (s32[2]{0:T(128)S(1)}, s32[2]{0:T(128)}, u32[]{:S(2)}) copy-start(s32[2]{0:T(128)} %constant.161) | copy-start | bytes 28
  10.8 19.8 %copy-start.49 = (f32[1,3,1024]{2,0,1:T(1,128)S(1)}, f32[1,3,1024]{2,0,1:T(1,128)}, u32[]{:S(2)}) copy-start(f32[1,3,1024]{2,0,1:T(1,128)} %param.13) | copy-start | bytes 36868
  10.8 19.8 %copy-start.50 = (s32[1024]{0:T(1024)S(1)}, s32[1024]{0:T(1024)}, u32[]{:S(2)}) copy-start(s32[1024]{0:T(1024)} %param.15) | copy-start | bytes 12292
  10.8 34.3 %collective-permute-start.1 = (f32[3,1,64,128]{3,2,1,0:T(8,128)S(1)}, f32[3,1,64,128]{3,2,1,0:T(8,128)S(1)}, u32[]{:S(2)}, u32[]{:S(2)}) collective-permute-start(f32[3,1,64,128]{3,2,1,0:T(8,128)S(1)} %get-tuple-element.70), channel_id=1, source_target_pairs={{0,1},{1,2},{2,3},{3,4},{4,5},{5,6},{6,7},{7,8},{8,9},{9,10},{10,1... | collective-permute-start | bytes 294920 | tf_op jit(solution)/shard_map/ppermute | solution.py:23
  14.1 35.1 %collective-permute-start = (f32[3,1,64,128]{3,2,1,0:T(8,128)S(1)}, f32[3,1,64,128]{3,2,1,0:T(8,128)}, u32[]{:S(2)}, u32[]{:S(2)}) collective-permute-start(f32[3,1,64,128]{3,2,1,0:T(8,128)S(1)} %get-tuple-element.69), channel_id=1, source_target_pairs={{1,0},{2,1},{3,2},{4,3},{5,4},{6,5},{7,6},{8,7},{9,8},{10,9},{11,1... | collective-permute-start | bytes 294920 | tf_op jit(solution)/shard_map/ppermute | solution.py:25
  30.8 14.4 %copy-start.6 = (f32[16,64,128]{2,1,0:T(8,128)S(1)}, f32[16,64,128]{2,1,0:T(8,128)}, u32[]{:S(2)}) copy-start(f32[16,64,128]{2,1,0:T(8,128)} %param.12) | copy-start | bytes 1572868
  38.2 15.9 %all-to-all-start = ((f32[32,4,128]{2,1,0:T(4,128)}), f32[32,4,128]{2,1,0:T(4,128)S(1)}, u32[]{:S(2)}, u32[]{:S(2)}) async-start(f32[32,4,128]{2,1,0:T(4,128)} %bitcast.38), calls=%async_computation | async-start | bytes 131072 | tf_op jit(solution)/shard_map/all_to_all | solution.py:92
  45.1 255.7 %all-reduce.58.cloned.1.call-start = ((), (), s32[]{:S(2)}) async-start(), calls=%async_computation.1 | async-start | bytes 3145728 | tf_op jit(solution)/shard_map/psum | solution.py:127
  51.0 12.4 %copy-start.8 = (f32[16,64,128]{2,1,0:T(8,128)}, f32[16,64,128]{2,1,0:T(8,128)S(1)}, u32[]{:S(2)}) copy-start(f32[16,64,128]{2,1,0:T(8,128)S(1)} %fusion.16) | copy-start | bytes 1572868
  51.0 10.5 %collective-permute-start.2 = (f32[3,1,64,128]{3,2,1,0:T(8,128)S(1)}, f32[3,1,64,128]{3,2,1,0:T(8,128)S(1)}, u32[]{:S(2)}, u32[]{:S(2)}) collective-permute-start(f32[3,1,64,128]{3,2,1,0:T(8,128)S(1)} %get-tuple-element.68), channel_id=1, source_target_pairs={{0,1},{1,2},{2,3},{3,4},{4,5},{5,6},{6,7},{7,8},{8,9},{9,10},{10,1... | collective-permute-start | bytes 294920 | tf_op jit(solution)/shard_map/ppermute | solution.py:23
  54.8 11.3 %collective-permute-start.3 = (f32[3,1,64,128]{3,2,1,0:T(8,128)S(1)}, f32[3,1,64,128]{3,2,1,0:T(8,128)S(1)}, u32[]{:S(2)}, u32[]{:S(2)}) collective-permute-start(f32[3,1,64,128]{3,2,1,0:T(8,128)S(1)} %get-tuple-element.67), channel_id=1, source_target_pairs={{1,0},{2,1},{3,2},{4,3},{5,4},{6,5},{7,6},{8,7},{9,8},{10,9},{11,1... | collective-permute-start | bytes 294920 | tf_op jit(solution)/shard_map/ppermute | solution.py:25
  69.0 36.1 %copy-start = (f32[16,64,128]{2,1,0:T(8,128)}, f32[16,64,128]{2,1,0:T(8,128)S(1)}, u32[]{:S(2)}) copy-start(f32[16,64,128]{2,1,0:T(8,128)S(1)} %get-tuple-element.21) | copy-start | bytes 1572868
  69.1 33.6 %collective-permute-start.4 = (f32[3,1,64,128]{3,2,1,0:T(8,128)S(1)}, f32[3,1,64,128]{3,2,1,0:T(8,128)S(1)}, u32[]{:S(2)}, u32[]{:S(2)}) collective-permute-start(f32[3,1,64,128]{3,2,1,0:T(8,128)S(1)} %get-tuple-element.65), channel_id=1, source_target_pairs={{1,0},{2,1},{3,2},{4,3},{5,4},{6,5},{7,6},{8,7},{9,8},{10,9},{11,1... | collective-permute-start | bytes 294920 | tf_op jit(solution)/shard_map/ppermute | solution.py:25
  74.3 30.4 %collective-permute-start.5 = (f32[3,1,64,128]{3,2,1,0:T(8,128)S(1)}, f32[3,1,64,128]{3,2,1,0:T(8,128)S(1)}, u32[]{:S(2)}, u32[]{:S(2)}) collective-permute-start(f32[3,1,64,128]{3,2,1,0:T(8,128)S(1)} %get-tuple-element.66), channel_id=1, source_target_pairs={{0,1},{1,2},{2,3},{3,4},{4,5},{5,6},{6,7},{7,8},{8,9},{9,10},{10,1... | collective-permute-start | bytes 294920 | tf_op jit(solution)/shard_map/ppermute | solution.py:23
  102.7 9.7 %slice-start.2 = ((s8[6291456]{0:T(1024)(128)(4,1)}), s8[4194304]{0:T(1024)(128)(4,1)S(1)}, s32[]{:S(2)}) async-start(s8[6291456]{0:T(1024)(128)(4,1)} %bitcast.381), calls=%async_computation.4 | async-start | bytes 8388608
  104.7 17.8 %copy-start.20 = (f32[16,64,128]{2,1,0:T(8,128)}, f32[16,64,128]{2,1,0:T(8,128)S(1)}, u32[]{:S(2)}) copy-start(f32[16,64,128]{2,1,0:T(8,128)S(1)} %fusion.36) | copy-start | bytes 1572868
  105.1 17.3 %copy-start.21 = (f32[16,64,128]{2,1,0:T(8,128)}, f32[16,64,128]{2,1,0:T(8,128)S(1)}, u32[]{:S(2)}) copy-start(f32[16,64,128]{2,1,0:T(8,128)S(1)} %fusion.41) | copy-start | bytes 1572868
  105.5 16.9 %copy-start.16 = (f32[16,64,128]{2,1,0:T(8,128)}, f32[16,64,128]{2,1,0:T(8,128)S(1)}, u32[]{:S(2)}) copy-start(f32[16,64,128]{2,1,0:T(8,128)S(1)} %fusion.50) | copy-start | bytes 1572868
  105.6 9.9 %collective-permute-start.7 = (f32[3,1,64,128]{3,2,1,0:T(8,128)S(1)}, f32[3,1,64,128]{3,2,1,0:T(8,128)S(1)}, u32[]{:S(2)}, u32[]{:S(2)}) collective-permute-start(f32[3,1,64,128]{3,2,1,0:T(8,128)S(1)} %get-tuple-element.63), channel_id=1, source_target_pairs={{1,0},{2,1},{3,2},{4,3},{5,4},{6,5},{7,6},{8,7},{9,8},{10,9},{11,1... | collective-permute-start | bytes 294920 | tf_op jit(solution)/shard_map/ppermute | solution.py:25
  110.1 10.0 %copy-start.1 = (f32[16,64,128]{2,1,0:T(8,128)S(1)}, f32[16,64,128]{2,1,0:T(8,128)}, u32[]{:S(2)}) copy-start(f32[16,64,128]{2,1,0:T(8,128)} %copy-done) | copy-start | bytes 1572868
  110.1 10.0 %copy-start.23 = (f32[16,64,128]{2,1,0:T(8,128)S(1)}, f32[16,64,128]{2,1,0:T(8,128)}, u32[]{:S(2)}) copy-start(f32[16,64,128]{2,1,0:T(8,128)} %copy-done.22) | copy-start | bytes 1572868
  110.1 10.0 %collective-permute-start.6 = (f32[3,1,64,128]{3,2,1,0:T(8,128)S(1)}, f32[3,1,64,128]{3,2,1,0:T(8,128)S(1)}, u32[]{:S(2)}, u32[]{:S(2)}) collective-permute-start(f32[3,1,64,128]{3,2,1,0:T(8,128)S(1)} %get-tuple-element.64), channel_id=1, source_target_pairs={{0,1},{1,2},{2,3},{3,4},{4,5},{5,6},{6,7},{7,8},{8,9},{9,10},{10,1... | collective-permute-start | bytes 294920 | tf_op jit(solution)/shard_map/ppermute | solution.py:23
  122.9 17.1 %copy-start.32 = (f32[16,64,128]{2,1,0:T(8,128)}, f32[16,64,128]{2,1,0:T(8,128)S(1)}, u32[]{:S(2)}) copy-start(f32[16,64,128]{2,1,0:T(8,128)S(1)} %fusion.134) | copy-start | bytes 1572868
  124.0 42.3 %collective-permute-start.8 = (f32[3,1,64,128]{3,2,1,0:T(8,128)}, f32[3,1,64,128]{3,2,1,0:T(8,128)S(1)}, u32[]{:S(2)}, u32[]{:S(2)}) collective-permute-start(f32[3,1,64,128]{3,2,1,0:T(8,128)} %get-tuple-element.60), channel_id=1, source_target_pairs={{1,0},{2,1},{3,2},{4,3},{5,4},{6,5},{7,6},{8,7},{9,8},{10,9},{11,1... | collective-permute-start | bytes 294920 | tf_op jit(solution)/shard_map/ppermute | solution.py:25
  127.3 39.1 %collective-permute-start.9 = (f32[3,1,64,128]{3,2,1,0:T(8,128)}, f32[3,1,64,128]{3,2,1,0:T(8,128)}, u32[]{:S(2)}, u32[]{:S(2)}) collective-permute-start(f32[3,1,64,128]{3,2,1,0:T(8,128)} %get-tuple-element.61), channel_id=1, source_target_pairs={{0,1},{1,2},{2,3},{3,4},{4,5},{5,6},{6,7},{7,8},{8,9},{9,10},{10,1... | collective-permute-start | bytes 294920 | tf_op jit(solution)/shard_map/ppermute | solution.py:23
  130.2 86.6 %collective-permute-start.12 = (f32[9,1,64,128]{3,2,0,1:T(8,128)}, f32[9,1,64,128]{3,2,0,1:T(8,128)S(1)}, u32[]{:S(2)}, u32[]{:S(2)}) collective-permute-start(f32[9,1,64,128]{3,2,0,1:T(8,128)} %get-tuple-element.38), channel_id=1, source_target_pairs={{0,1},{1,2},{2,3},{3,4},{4,5},{5,6},{6,7},{7,8},{8,9},{9,10},{10,1... | collective-permute-start | bytes 884744 | tf_op jit(solution)/shard_map/ppermute | solution.py:23
  132.1 93.2 %collective-permute-start.13 = (f32[9,1,64,128]{3,2,0,1:T(8,128)}, f32[9,1,64,128]{3,2,0,1:T(8,128)}, u32[]{:S(2)}, u32[]{:S(2)}) collective-permute-start(f32[9,1,64,128]{3,2,0,1:T(8,128)} %get-tuple-element.37), channel_id=1, source_target_pairs={{1,0},{2,1},{3,2},{4,3},{5,4},{6,5},{7,6},{8,7},{9,8},{10,9},{11,1... | collective-permute-start | bytes 884744 | tf_op jit(solution)/shard_map/ppermute | solution.py:25
  166.4 10.6 %slice-start.4 = ((s8[6291456]{0:T(1024)(128)(4,1)}), s8[4194304]{0:T(1024)(128)(4,1)S(1)}, s32[]{:S(2)}) async-start(s8[6291456]{0:T(1024)(128)(4,1)} %bitcast.383), calls=%async_computation.6 | async-start | bytes 8388608
  166.4 10.6 %slice-start.5 = ((s8[6291456]{0:T(1024)(128)(4,1)}), s8[2097152]{0:T(1024)(128)(4,1)S(1)}, s32[]{:S(2)}) async-start(s8[6291456]{0:T(1024)(128)(4,1)} %bitcast.383), calls=%async_computation.7 | async-start | bytes 4194304
  174.9 12.2 %copy-start.24 = (f32[16,64,128]{2,1,0:T(8,128)S(1)}, f32[16,64,128]{2,1,0:T(8,128)}, u32[]{:S(2)}) copy-start(f32[16,64,128]{2,1,0:T(8,128)} %copy-done.22) | copy-start | bytes 1572868
  174.9 12.2 %collective-permute-start.10 = (f32[3,1,64,128]{3,2,1,0:T(8,128)S(1)}, f32[3,1,64,128]{3,2,1,0:T(8,128)}, u32[]{:S(2)}, u32[]{:S(2)}) collective-permute-start(f32[3,1,64,128]{3,2,1,0:T(8,128)S(1)} %get-tuple-element.59), channel_id=1, source_target_pairs={{0,1},{1,2},{2,3},{3,4},{4,5},{5,6},{6,7},{7,8},{8,9},{9,10},{10,1... | collective-permute-start | bytes 294920 | tf_op jit(solution)/shard_map/ppermute | solution.py:23
  179.2 46.1 %collective-permute-start.11 = (f32[3,1,64,128]{3,2,1,0:T(8,128)S(1)}, f32[3,1,64,128]{3,2,1,0:T(8,128)}, u32[]{:S(2)}, u32[]{:S(2)}) collective-permute-start(f32[3,1,64,128]{3,2,1,0:T(8,128)S(1)} %get-tuple-element.58), channel_id=1, source_target_pairs={{1,0},{2,1},{3,2},{4,3},{5,4},{6,5},{7,6},{8,7},{9,8},{10,9},{11,1... | collective-permute-start | bytes 294920 | tf_op jit(solution)/shard_map/ppermute | solution.py:25
  216.8 8.5 %slice-start = ((s8[4718592]{0:T(1024)(128)(4,1)}), s8[4194304]{0:T(1024)(128)(4,1)S(1)}, s32[]{:S(2)}) async-start(s8[4718592]{0:T(1024)(128)(4,1)} %bitcast.360), calls=%async_computation.2 | async-start | bytes 8388608
  216.8 8.5 %slice-start.1 = ((s8[4718592]{0:T(1024)(128)(4,1)}), s8[524288]{0:T(1024)(128)(4,1)S(1)}, s32[]{:S(2)}) async-start(s8[4718592]{0:T(1024)(128)(4,1)} %bitcast.360), calls=%async_computation.3 | async-start | bytes 1048576
  216.8 8.5 %copy-start.2 = (f32[16,64,128]{2,1,0:T(8,128)S(1)}, f32[16,64,128]{2,1,0:T(8,128)}, u32[]{:S(2)}) copy-start(f32[16,64,128]{2,1,0:T(8,128)} %copy-done) | copy-start | bytes 1572868
  216.9 8.8 %copy-start.36 = (f32[16,64,128]{2,1,0:T(8,128)S(1)}, f32[16,64,128]{2,1,0:T(8,128)}, u32[]{:S(2)}) copy-start(f32[16,64,128]{2,1,0:T(8,128)} %get-tuple-element.48) | copy-start | bytes 1572868
  216.9 8.9 %copy-start.38 = (f32[16,64,128]{2,1,0:T(8,128)S(1)}, f32[16,64,128]{2,1,0:T(8,128)}, u32[]{:S(2)}) copy-start(f32[16,64,128]{2,1,0:T(8,128)} %get-tuple-element.29) | copy-start | bytes 1572868
  216.9 9.1 %copy-start.39 = (f32[16,64,128]{2,1,0:T(8,128)S(1)}, f32[16,64,128]{2,1,0:T(8,128)}, u32[]{:S(2)}) copy-start(f32[16,64,128]{2,1,0:T(8,128)} %get-tuple-element.30) | copy-start | bytes 1572868
  242.2 68.1 %copy-start.46 = (f32[16,64,128]{2,1,0:T(8,128)S(1)}, f32[16,64,128]{2,1,0:T(8,128)}, u32[]{:S(2)}) copy-start(f32[16,64,128]{2,1,0:T(8,128)} %get-tuple-element.7) | copy-start | bytes 1572868
  301.8 9.4 %collective-permute-start.14 = (f32[3,1,64,128]{3,2,1,0:T(8,128)S(1)}, f32[3,1,64,128]{3,2,1,0:T(8,128)S(1)}, u32[]{:S(2)}, u32[]{:S(2)}) collective-permute-start(f32[3,1,64,128]{3,2,1,0:T(8,128)S(1)} %get-tuple-element.56), channel_id=1, source_target_pairs={{1,0},{2,1},{3,2},{4,3},{5,4},{6,5},{7,6},{8,7},{9,8},{10,9},{11,1... | collective-permute-start | bytes 294920 | tf_op jit(solution)/shard_map/ppermute | solution.py:25
  308.4 10.2 %collective-permute-start.15 = (f32[3,1,64,128]{3,2,1,0:T(8,128)S(1)}, f32[3,1,64,128]{3,2,1,0:T(8,128)S(1)}, u32[]{:S(2)}, u32[]{:S(2)}) collective-permute-start(f32[3,1,64,128]{3,2,1,0:T(8,128)S(1)} %get-tuple-element.57), channel_id=1, source_target_pairs={{0,1},{1,2},{2,3},{3,4},{4,5},{5,6},{6,7},{7,8},{8,9},{9,10},{10,1... | collective-permute-start | bytes 294920 | tf_op jit(solution)/shard_map/ppermute | solution.py:23
  311.2 19.2 %copy-start.45 = (f32[16,64,128]{2,1,0:T(8,128)S(1)}, f32[16,64,128]{2,1,0:T(8,128)}, u32[]{:S(2)}) copy-start(f32[16,64,128]{2,1,0:T(8,128)} %get-tuple-element.6) | copy-start | bytes 1572868
  325.1 6.2 %collective-permute-start.16 = (f32[3,1,64,128]{3,2,1,0:T(8,128)S(1)}, f32[3,1,64,128]{3,2,1,0:T(8,128)S(1)}, u32[]{:S(2)}, u32[]{:S(2)}) collective-permute-start(f32[3,1,64,128]{3,2,1,0:T(8,128)S(1)} %get-tuple-element.54), channel_id=1, source_target_pairs={{1,0},{2,1},{3,2},{4,3},{5,4},{6,5},{7,6},{8,7},{9,8},{10,9},{11,1... | collective-permute-start | bytes 294920 | tf_op jit(solution)/shard_map/ppermute | solution.py:25
  327.0 9.9 %collective-permute-start.17 = (f32[3,1,64,128]{3,2,1,0:T(8,128)S(1)}, f32[3,1,64,128]{3,2,1,0:T(8,128)S(1)}, u32[]{:S(2)}, u32[]{:S(2)}) collective-permute-start(f32[3,1,64,128]{3,2,1,0:T(8,128)S(1)} %get-tuple-element.55), channel_id=1, source_target_pairs={{0,1},{1,2},{2,3},{3,4},{4,5},{5,6},{6,7},{7,8},{8,9},{9,10},{10,1... | collective-permute-start | bytes 294920 | tf_op jit(solution)/shard_map/ppermute | solution.py:23
  (31 other events, 143.2 us)
Sparse Core Ops, SparseCore 0:
  239.5 61.2 all-reduce.57
where the time goes:
time: 349 us; the launch traced here: 346 us
  other arithmetic  150 us (43%)
  starting transfers between devices  79.3 us (23%)
  waiting for transfers between devices  73 us (21%)
  local copies, waits for them, and re-layouts  28.3 us (8%)
  between operations  15.3 us (4%)
    scatter-add x3, other arithmetic, local(): fields[5].reshape(-1).at[targets].add(arrived[:, step, :].reshape(-1))  79.2 us
    psum x1, waiting for transfers between devices, local(): grad = lax.psum(terms, 'shot')  55.3 us
    ppermute x9, starting transfers between devices, with_halo(): lax.ppermute(head, axis, [((i + 1) % count, i) for i in range(ends)])  50.6 us
    another operation x4, other arithmetic, local(): terms = jnp.stack([glam, gmu, grho])  30.1 us
    ppermute x9, starting transfers between devices, with_halo(): lax.ppermute(tail, axis, [(i, (i + 1) % count) for i in range(ends)])  21.7 us
    ppermute x9, waiting for transfers between devices, with_halo(): lax.ppermute(tail, axis, [(i, (i + 1) % count) for i in range(ends)])  17.7 us
    unnamed x130, local copies, waits for them, and re-layouts  16.4 us
    another operation x2, other arithmetic  9.04 us
  transfers between devices with their start and end apart: 20, of which 4 were waited for; matrix products, arithmetic and copies ran while one was open for 41% of the time, Pallas kernels for 0%

commit v1 on v0

v1 whole, which is shorter than its diff:
```python
import functools

import jax
import jax.numpy as jnp
from jax import lax
from jax.experimental import pallas as pl
from jax.experimental.pallas import tpu as pltpu
from jax.sharding import PartitionSpec as P

STEPS = 3
CX, NY, NZ = 16, 64, 128
NX = 512
N_SPACE = 32
CH_DEV = 1024
CAP = 128
COURANT = 0.3
KAPPA = 0.15
ROWS = 32
PAD = 8
PY = NY + 2 * PAD
VX, VY, VZ, SXX, SYY, SZZ, SXY, SXZ, SYZ = range(9)
CHUNKS = (0, 3, 1, 2)
F32, BF16, I32 = jnp.float32, jnp.bfloat16, jnp.int32


def nt(a, b):
    return lax.dot_general(a, b, (((1,), (1,)), ((), ())), preferred_element_type=F32)


def lane_of(rows):
    return lax.broadcasted_iota(I32, (rows, NZ), 1)


def zminus(f):
    rolled = pltpu.roll(f, 1, 1)
    return f - jnp.where(lane_of(f.shape[0]) == 0, 0.0, rolled)


def zplus(f):
    rolled = pltpu.roll(f, NZ - 1, 1)
    return jnp.where(lane_of(f.shape[0]) == NZ - 1, 0.0, rolled) - f


def kernel(
    adj, fwd, vp_h, sr_h, dn_h, res, own, cell,
    out_adj, out_grad,
    f0, f1, f2, f3, f4, f5, f6, f7, f8,
    fw, dense, cb, cl, cm, g0, g1, g2,
    packed, arrived, a_one, b_one,
    gs, rb1, s2, rb2, h0, h1, og,
    load_f, load_w, load_p, out_sem,
    halo_s, halo_r, fh_s, fh_r, a2a_s, a2a_r,
    r1_s, r1_r, r2_s, r2_r, gx_s, gx_r,
):
    F = (f0, f1, f2, f3, f4, f5, f6, f7, f8)
    G = (g0, g1, g2)
    me = lax.axis_index("space")
    sh = lax.axis_index("shot")
    core = sh % 2
    chip = sh // 2
    has_left = me > 0
    has_right = me < N_SPACE - 1
    left = (me + N_SPACE - 1) % N_SPACE
    right = (me + 1) % N_SPACE
    mate = 2 * chip + (1 - core)
    cross = 2 * (1 - chip) + core
    inner = pl.ds(PAD, NY)

    loads_p = [pltpu.make_async_copy(src, dst, load_p.at[i]) for i, (src, dst) in enumerate(((vp_h, cl), (sr_h, cm), (dn_h, cb)))]
    loads_f = [pltpu.make_async_copy(adj.at[0, k], F[k].at[pl.ds(1, CX), inner], load_f.at[k]) for k in range(9)]
    loads_w = [pltpu.make_async_copy(fwd.at[0, t], fw.at[t, :, pl.ds(1, CX), inner], load_w.at[t]) for t in range(STEPS + 1)]
    for c in loads_p:
        c.start()
    for k in (SXX, SXY, SXZ, SYY, SYZ, SZZ, VX, VY, VZ):
        loads_f[k].start()
    for c in loads_w:
        c.start()

    zpad = jnp.zeros((PAD, NZ), F32)

    def zero_pads(x, carry):
        for k in (VX, VY, VZ, SYY, SXY, SYZ):
            F[k][x, pl.ds(0, PAD), :] = zpad
            F[k][x, pl.ds(PAD + NY, PAD), :] = zpad
        for t in range(STEPS):
            for k in range(3):
                fw[t, k, x, pl.ds(0, PAD), :] = zpad
                fw[t, k, x, pl.ds(PAD + NY, PAD), :] = zpad
        return carry

    lax.fori_loop(1, CX + 1, zero_pads, 0)

    def zero_h(x, carry):
        for k in range(3):
            h0[k, x, :, :] = jnp.zeros((40, NZ), F32)
        return carry

    lax.fori_loop(0, CX + 4, zero_h, 0)

    def zero_gs(i, carry):
        for k in range(3):
            for xx in range(2):
                gs[0, k, i, pl.ds(20 * xx, 2), :] = jnp.zeros((2, NZ), F32)
                gs[3, k, i, pl.ds(20 * xx + 18, 2), :] = jnp.zeros((2, NZ), F32)
        return carry

    lax.fori_loop(0, CX // 2, zero_gs, 0)
    zplane = jnp.zeros((NY, NZ), F32)

    @pl.when(me == 0)
    def _():
        for k in (VX, SXY, SXZ):
            F[k][0, inner, :] = zplane
        for t in range(STEPS):
            fw[t, 0, 0, inner, :] = zplane

    @pl.when(me == N_SPACE - 1)
    def _():
        for k in (SXX, VY, VZ):
            F[k][CX + 1, inner, :] = zplane
        for t in range(STEPS):
            for k in (1, 2):
                fw[t, k, CX + 1, inner, :] = zplane

    barrier = pltpu.get_barrier_semaphore()

    def greet(k, carry):
        pl.semaphore_signal(barrier, inc=1, device_id={"space": (me + k) % N_SPACE}, device_id_type=pl.DeviceIdType.MESH)
        return carry

    lax.fori_loop(1, N_SPACE, greet, 0)
    for other in (mate, cross):
        pl.semaphore_signal(barrier, inc=1, device_id={"shot": other}, device_id_type=pl.DeviceIdType.MESH)

    blk = 256
    upper = (lax.broadcasted_iota(I32, (blk, blk), 0) < lax.broadcasted_iota(I32, (blk, blk), 1)).astype(F32).astype(BF16)
    carry_n = jnp.zeros((N_SPACE, 1), F32)
    acc = jnp.zeros((N_SPACE * 16, CAP), F32)
    for b in range(CH_DEV // blk):
        lanes = pl.ds(b * blk, blk)
        o = own[:, lanes]
        oh = (o == lax.broadcasted_iota(I32, (N_SPACE, blk), 0)).astype(F32)
        ranks = jnp.dot(oh.astype(BF16), upper, preferred_element_type=F32) + carry_n
        carry_n = carry_n + jnp.sum(oh, axis=1, keepdims=True)
        rank = jnp.sum(oh * ranks, axis=0, keepdims=True)
        slot = (rank.astype(I32) == lax.broadcasted_iota(I32, (CAP, blk), 0)).astype(F32).astype(BF16)
        cl_ = cell[:, lanes]
        r = [res[t, :, lanes] for t in range(STEPS)]
        hi = [v.astype(BF16).astype(F32) for v in r]
        zero = jnp.zeros((1, blk), F32)
        rows = (
            hi
            + [(cl_ >> 13).astype(F32), ((cl_ >> 7) & 63).astype(F32), (cl_ & 127).astype(F32), zero, zero]
            + [a - h for a, h in zip(r, hi)]
            + [zero] * 5
        )
        payload = jnp.concatenate(rows, axis=0)
        lhs = (oh[:, None, :] * payload[None, :, :]).reshape(N_SPACE * 16, blk).astype(BF16)
        acc = acc + nt(lhs, slot)
    acc = acc.reshape(N_SPACE, 16, CAP)
    packed[...] = acc[:, :8, :] + acc[:, 8:, :]

    pl.semaphore_wait(barrier, N_SPACE + 1)

    def send(src, dst, s, r, to):
        return pltpu.make_async_remote_copy(
            src_ref=src, dst_ref=dst, send_sem=s, recv_sem=r, device_id={"space": to}, device_id_type=pl.DeviceIdType.MESH
        )

    def tail_to_right(step, j, k, src=None):
        src = F[k].at[CX, inner] if src is None else src
        return send(src, F[k].at[0, inner], halo_s.at[step, j], halo_r.at[step, j], right)

    def head_to_left(step, j, k, src=None):
        src = F[k].at[1, inner] if src is None else src
        return send(src, F[k].at[CX + 1, inner], halo_s.at[step, j], halo_r.at[step, j], left)

    def stress_halo(step):
        hb = step == 0
        to_left = [head_to_left(step, 0, SXX, adj.at[0, SXX, 0] if hb else None)]
        to_right = [
            tail_to_right(step, 1, SXY, adj.at[0, SXY, CX - 1] if hb else None),
            tail_to_right(step, 2, SXZ, adj.at[0, SXZ, CX - 1] if hb else None),
        ]
        return to_left, to_right

    def speed_halo(step):
        return [head_to_left(step, 3, VY), head_to_left(step, 4, VZ)], [tail_to_right(step, 5, VX)]

    def forward_halo():
        return (
            [send(fwd.at[0, pl.ds(0, STEPS), pl.ds(1, 2), 0], fw.at[pl.ds(0, STEPS), pl.ds(1, 2), CX + 1, inner], fh_s.at[0], fh_r.at[0], left)],
            [send(fwd.at[0, pl.ds(0, STEPS), 0, CX - 1], fw.at[pl.ds(0, STEPS), 0, 0, inner], fh_s.at[1], fh_r.at[1], right)],
        )

    def start(pair):
        @pl.when(has_left)
        def _():
            for c in pair[0]:
                c.start()

        @pl.when(has_right)
        def _():
            for c in pair[1]:
                c.start()

    def wait_recv(pair):
        @pl.when(has_right)
        def _():
            for c in pair[0]:
                c.wait_recv()

        @pl.when(has_left)
        def _():
            for c in pair[1]:
                c.wait_recv()

    def wait_send(pair):
        @pl.when(has_left)
        def _():
            for c in pair[0]:
                c.wait_send()

        @pl.when(has_right)
        def _():
            for c in pair[1]:
                c.wait_send()

    start(stress_halo(0))

    def channel_copy(k):
        to = (me + k) % N_SPACE
        return send(packed.at[to], arrived.at[me], a2a_s.at[k], a2a_r.at[k], to)

    def channel_start(k, carry):
        channel_copy(k).start()
        return carry

    lax.fori_loop(1, N_SPACE, channel_start, 0)
    start(forward_halo())
    arrived[me] = packed[me]

    for c in loads_p:
        c.wait()

    def params(x, carry):
        rho, vp, ratio = cb[x], cl[x], cm[x]
        vs = ratio * vp
        mu = rho * vs * vs
        cb[x] = COURANT * (1.0 / rho)
        cl[x] = COURANT * (rho * vp * vp - 2.0 * mu)
        cm[x] = COURANT * mu
        return carry

    lax.fori_loop(0, CX, params, 0)
    for c in loads_f:
        c.wait()

    def speeds(x, carry=0):
        for y in range(0, NY, ROWS):
            def at(k, dx=0, dy=0):
                return F[k][x + dx, pl.ds(PAD + y + dy, ROWS), :]

            here = pl.ds(PAD + y, ROWS)
            b = cb[x - 1, pl.ds(y, ROWS), :]
            sxy, sxz, syz = at(SXY), at(SXZ), at(SYZ)
            vx = at(VX) + b * ((at(SXX, 1) - at(SXX)) + (sxy - at(SXY, 0, -1)) + zminus(sxz))
            vy = at(VY) + b * ((sxy - at(SXY, -1)) + (at(SYY, 0, 1) - at(SYY)) + zminus(syz))
            vz = at(VZ) + b * ((sxz - at(SXZ, -1)) + (syz - at(SYZ, 0, -1)) + zplus(at(SZZ)))
            F[VX][x, here, :] = vx
            F[VY][x, here, :] = vy
            F[VZ][x, here, :] = vz
        return carry

    def stresses(step, x, carry=0):
        for y in range(0, NY, ROWS):
            def at(k, dx=0, dy=0):
                return F[k][x + dx, pl.ds(PAD + y + dy, ROWS), :]

            here = pl.ds(PAD + y, ROWS)
            flat = pl.ds(y, ROWS)
            lam, mu = cl[x - 1, flat, :], cm[x - 1, flat, :]
            vx, vy, vz = at(VX), at(VY), at(VZ)
            exx = vx - at(VX, -1)
            eyy = vy - at(VY, 0, -1)
            ezz = zminus(vz)
            base = lam * (exx + eyy + ezz)
            mu2 = mu + mu
            F[SXX][x, here, :] = at(SXX) + (base + mu2 * exx)
            F[SYY][x, here, :] = at(SYY) + (base + mu2 * eyy)
            F[SZZ][x, here, :] = at(SZZ) + (base + mu2 * ezz)
            F[SXY][x, here, :] = at(SXY) + mu * ((at(VY, 1) - vy) + (at(VX, 0, 1) - vx))
            F[SXZ][x, here, :] = at(SXZ) + mu * ((at(VZ, 1) - vz) + zplus(vx))
            F[SYZ][x, here, :] = at(SYZ) + mu * ((at(VZ, 0, 1) - vz) + zplus(vy))
        return carry

    def gradients(step, x, carry=0):
        for y in range(0, NY, ROWS):
            def at(k):
                return F[k][x, pl.ds(PAD + y, ROWS), :]

            def u(k, dx=0, dy=0):
                return fw[step, k, x + dx, pl.ds(PAD + y + dy, ROWS), :]

            def w(k):
                return fw[step + 1, k, x, pl.ds(PAD + y, ROWS), :]

            here = pl.ds(PAD + y, ROWS)
            flat = pl.ds(y, ROWS)
            sxx, syy = at(SXX), at(SYY)
            szz = at(SZZ) + dense[step, x - 1, flat, :]
            F[SZZ][x, here, :] = szz
            ux, uy, uz = u(0), u(1), u(2)
            fxx = ux - u(0, -1)
            fyy = uy - u(1, 0, -1)
            fzz = zminus(uz)
            lam = (fxx + fyy + fzz) * (sxx + syy + szz)
            mu = (
                2.0 * (fxx * sxx + fyy * syy + fzz * szz)
                + ((u(1, 1) - uy) + (u(0, 0, 1) - ux)) * at(SXY)
                + ((u(2, 1) - uz) + zplus(ux)) * at(SXZ)
                + ((u(2, 0, 1) - uz) + zplus(uy)) * at(SYZ)
            )
            rho = at(VX) * (w(0) - ux) + at(VY) * (w(1) - uy) + at(VZ) * (w(2) - uz)
            for ref, term in zip(G, (lam, mu, rho)):
                ref[x - 1, flat, :] = term if step == 0 else ref[x - 1, flat, :] + term
        return carry

    def densify():
        def channel_wait(k, carry):
            channel_copy(k).wait_recv()
            return carry

        lax.fori_loop(1, N_SPACE, channel_wait, 0)

        def one_hot(s, carry):
            lanes = pl.ds(pl.multiple_of(s * CAP, CAP), CAP)
            row = arrived[s]
            x, y, z = row[3:4].astype(I32), row[4:5].astype(I32), row[5:6].astype(I32)
            yone = (y == lax.broadcasted_iota(I32, (NY, CAP), 0)).astype(F32)
            zone = (z == lax.broadcasted_iota(I32, (NZ, CAP), 0)).astype(F32)
            for i in range(CX):
                a_one[pl.ds(i * NY, NY), lanes] = jnp.where(x == i, yone, 0.0).astype(BF16)
            for t in range(STEPS):
                v = row[t : t + 1]
                hi = v.astype(BF16).astype(F32)
                b_one[pl.ds(2 * t * NZ, NZ), lanes] = (zone * hi).astype(BF16)
                b_one[pl.ds((2 * t + 1) * NZ, NZ), lanes] = (zone * (v - hi)).astype(BF16)
            return carry

        lax.fori_loop(0, N_SPACE, one_hot, 0)

        def product(m, carry):
            got = nt(a_one[pl.ds(pl.multiple_of(m * 256, 256), 256), :], b_one[...])
            for t in range(STEPS):
                both = got[:, 2 * t * NZ : (2 * t + 1) * NZ] + got[:, (2 * t + 1) * NZ : (2 * t + 2) * NZ]
                dense[t, pl.ds(4 * m, 4), :, :] = both.reshape(4, NY, NZ)
            return carry

        lax.fori_loop(0, 4, product, 0)

    for step in range(STEPS):
        if step > 0:
            wait_send(speed_halo(step - 1))
        lax.fori_loop(2, CX, speeds, 0)
        wait_recv(stress_halo(step))
        speeds(1)
        speeds(CX)
        start(speed_halo(step))
        wait_send(stress_halo(step))
        lax.fori_loop(2, CX, functools.partial(stresses, step), 0)
        wait_recv(speed_halo(step))
        stresses(step, 1)
        stresses(step, CX)
        if step + 1 < STEPS:
            start(stress_halo(step + 1))
        if step == 0:
            densify()
            for c in loads_w:
                c.wait()
            wait_recv(forward_halo())
        lax.fori_loop(1, CX + 1, functools.partial(gradients, step), 0)
    wait_send(speed_halo(STEPS - 1))
    wait_send(forward_halo())

    def channel_sent(k, carry):
        channel_copy(k).wait_send()
        return carry

    lax.fori_loop(1, N_SPACE, channel_sent, 0)
    stores = [pltpu.make_async_copy(F[k].at[pl.ds(1, CX), inner], out_adj.at[0, k], out_sem.at[k]) for k in range(9)]
    for c in stores:
        c.start()

    def to_mate(ch):
        return [
            pltpu.make_async_remote_copy(
                src_ref=gs.at[2 * j + 1 - core, :, pl.ds(2 * ch, 2)],
                dst_ref=rb1.at[j, :, pl.ds(2 * ch, 2)],
                send_sem=r1_s.at[ch, j],
                recv_sem=r1_r.at[ch, j],
                device_id={"shot": mate},
                device_id_type=pl.DeviceIdType.MESH,
            )
            for j in range(2)
        ]

    def to_cross(ch):
        return pltpu.make_async_remote_copy(
            src_ref=s2.at[:, pl.ds(2 * ch, 2)],
            dst_ref=rb2.at[:, pl.ds(2 * ch, 2)],
            send_sem=r2_s.at[ch],
            recv_sem=r2_r.at[ch],
            device_id={"shot": cross},
            device_id_type=pl.DeviceIdType.MESH,
        )

    def slabs(i, carry):
        for k in range(3):
            for xx in range(2):
                for s in range(4):
                    lo, hi = max(0, 16 * s - 2), min(NY, 16 * s + 18)
                    off = 20 * xx + lo - (16 * s - 2)
                    gs[s, k, i, pl.ds(off, hi - lo), :] = G[k][2 * i + xx, pl.ds(lo, hi - lo), :]
        return carry

    for ch in CHUNKS:
        lax.fori_loop(2 * ch, 2 * ch + 2, slabs, 0)
        for c in to_mate(ch):
            c.start()

    def sum_cross(i, carry):
        for k in range(3):
            s2[k, i] = gs[2 * (1 - chip) + core, k, i] + rb1[1 - chip, k, i]
        return carry

    for ch in CHUNKS:
        for c in to_mate(ch):
            c.wait_recv()
        lax.fori_loop(2 * ch, 2 * ch + 2, sum_cross, 0)
        to_cross(ch).start()

    def sum_own(i, carry):
        for k in range(3):
            for xx in range(2):
                part = pl.ds(20 * xx, 20)
                total = (gs[2 * chip + core, k, i, part, :] + rb1[chip, k, i, part, :]) + rb2[k, i, part, :]
                h0[k, 2 + 2 * i + xx, pl.ds(8, 20), :] = total
        return carry

    rim = pl.ds(8, 24)
    grad_halo = (
        [send(h0.at[:, pl.ds(2, 2), rim], h0.at[:, pl.ds(CX + 2, 2), rim], gx_s.at[0], gx_r.at[0], left)],
        [send(h0.at[:, pl.ds(CX, 2), rim], h0.at[:, pl.ds(0, 2), rim], gx_s.at[1], gx_r.at[1], right)],
    )
    for n, ch in enumerate(CHUNKS):
        to_cross(ch).wait_recv()
        lax.fori_loop(2 * ch, 2 * ch + 2, sum_own, 0)
        if n == 1:
            start(grad_halo)
    wait_recv(grad_halo)
    wait_send(grad_halo)

    def near(h, k, p, lo, n):
        def at(dp=0, dy=0):
            return h[k, p + dp, pl.ds(lo + dy, n), :]

        mid = at()
        lane = lane_of(n)
        total = at(1) + at(-1) + at(0, 1) + at(0, -1)
        total = total + jnp.where(lane == NZ - 1, 0.0, pltpu.roll(mid, NZ - 1, 1)) + jnp.where(lane == 0, 0.0, pltpu.roll(mid, 1, 1))
        return mid + KAPPA * (total - 6.0 * mid)

    def sweep_one(p, carry):
        gx = CX * me + p - 2
        gy = 16 * sh - 2 + lax.broadcasted_iota(I32, (24, NZ), 0)
        keep = (gy >= 0) & (gy < NY) & (gx >= 0) & (gx < NX)
        for k in range(3):
            h1[k, p, rim, :] = jnp.where(keep, near(h0, k, p, 8, 24), 0.0)
        return carry

    lax.fori_loop(1, CX + 3, sweep_one, 0)

    def sweep_two(x, carry):
        for k in range(3):
            og[k, x] = near(h1, k, x + 2, 10, 16)
        return carry

    lax.fori_loop(0, CX, sweep_two, 0)
    grad_out = pltpu.make_async_copy(og, out_grad, out_sem.at[9])
    grad_out.start()
    for ch in CHUNKS:
        for c in to_mate(ch):
            c.wait_send()
        to_cross(ch).wait_send()
    for c in stores:
        c.wait()
    grad_out.wait()


def local(adjoint_state, forward_velocity, vp, shear_ratio, density, residuals, owner, cell):
    res = residuals.reshape(STEPS, 1, CH_DEV)
    own = owner.reshape(1, CH_DEV)
    cells = cell.reshape(1, CH_DEV)
    hbm = pl.BlockSpec(memory_space=pl.ANY)
    vmem = pl.BlockSpec(memory_space=pltpu.VMEM)
    volume = pltpu.VMEM((CX, NY, NZ), F32)
    dma = pltpu.SemaphoreType.DMA
    scratch = (
        [pltpu.VMEM((CX + 2, PY, NZ), F32)] * 9
        + [
            pltpu.VMEM((STEPS + 1, 3, CX + 2, PY, NZ), F32),
            pltpu.VMEM((STEPS, CX, NY, NZ), F32),
        ]
        + [volume] * 6
        + [
            pltpu.VMEM((N_SPACE, 8, CAP), F32),
            pltpu.VMEM((N_SPACE, 8, CAP), F32),
            pltpu.VMEM((CX * NY, N_SPACE * CAP), BF16),
            pltpu.VMEM((2 * STEPS * NZ, N_SPACE * CAP), BF16),
            pltpu.VMEM((4, 3, CX // 2, 40, NZ), F32),
            pltpu.VMEM((2, 3, CX // 2, 40, NZ), F32),
            pltpu.VMEM((3, CX // 2, 40, NZ), F32),
            pltpu.VMEM((3, CX // 2, 40, NZ), F32),
            pltpu.VMEM((3, CX + 4, 40, NZ), F32),
            pltpu.VMEM((3, CX + 4, 40, NZ), F32),
            pltpu.VMEM((3, CX, 16, NZ), F32),
        ]
        + [dma((9,)), dma((4,)), dma((3,)), dma((10,))]
        + [dma((STEPS, 6)), dma((STEPS, 6)), dma((2,)), dma((2,)), dma((N_SPACE,)), dma((N_SPACE,))]
        + [dma((4, 2)), dma((4, 2)), dma((4,)), dma((4,)), dma((2,)), dma((2,))]
    )
    return pl.pallas_call(
        kernel,
        out_shape=(
            jax.ShapeDtypeStruct((1, 9, CX, NY, NZ), F32),
            jax.ShapeDtypeStruct((3, CX, 16, NZ), F32),
        ),
        in_specs=[hbm] * 5 + [vmem] * 3,
        out_specs=(hbm, hbm),
        scratch_shapes=scratch,
        compiler_params=pltpu.CompilerParams(collective_id=0, has_side_effects=True, vmem_limit_bytes=60 * 1024 * 1024),
    )(adjoint_state, forward_velocity, vp, shear_ratio, density, res, own, cells)


def solution(mesh):
    in_specs = (
        P("shot", None, "space", None, None),
        P("shot", None, None, "space", None, None),
        P("space", None, None),
        P("space", None, None),
        P("space", None, None),
        P("shot", None, "space"),
        P("space", None),
        P("space"),
    )
    out_specs = (P("shot", None, "space", None, None), P(None, "space", "shot", None))
    return jax.shard_map(local, mesh=mesh, in_specs=in_specs, out_specs=out_specs, check_vma=False)
```

time: 349 us -> 80.9 us (0.23)
  other arithmetic: 150 us -> 0 us
  starting transfers between devices: 79.3 us -> 0 us
  Pallas kernels: 0 us -> 74 us
  waiting for transfers between devices: 73 us -> 0 us
  local copies, waits for them, and re-layouts: 28.3 us -> 6.04 us
  between operations: 15.3 us -> 0.65 us
    scatter-add x3 -> x0, other arithmetic: 79.2 us -> none  [local(): fields[5].reshape(-1).at[targets].add(arrived[:, step, :].reshape(-1))]
    pallas_call x0 -> x1, Pallas kernels: none -> 74 us  [local(): pl.pallas_call(kernel, out_shape=(jax.ShapeDtypeStruct((1, 9, CX, NY, NZ)...]
    ppermute x18 -> x0, starting transfers between devices: 72.3 us -> none  [the longest x9 50.6 us: with_halo(): lax.ppermute(head, axis, [((i + 1) % count, i) for i in range(ends)])]
    psum x1 -> x0, waiting for transfers between devices: 55.3 us -> none  [local(): grad = lax.psum(terms, 'shot')]
    another operation x9 -> x0, other arithmetic: 39.2 us -> none  [the longest x4 30.1 us: local(): terms = jnp.stack([glam, gmu, grho])]
    add x16 -> x0, other arithmetic: 30.7 us -> none  [the longest x2 7.46 us: local(): grad = grad + KAPPA * (near - 6.0 * grad)]
    ppermute x18 -> x0, waiting for transfers between devices: 17.7 us -> none  [the longest x9 17.7 us: with_halo(): lax.ppermute(tail, axis, [(i, (i + 1) % count) for i in range(ends)])]
    unnamed x130 -> x4, local copies, waits for them, and re-layouts: 16.4 us -> 6.04 us
  transfers between devices with their start and end apart: 20 -> 0, of which waited for: 4 -> 0; matrix products, arithmetic and copies ran while one was open for 41% -> 0% of each run, Pallas kernels for 0% -> 0%
where the time goes in v1:
time: 80.9 us; the launch traced here: 80.7 us
  Pallas kernels  74 us (91%)
  local copies, waits for them, and re-layouts  6.04 us (7%)
    pallas_call x1, Pallas kernels, local(): pl.pallas_call(kernel, out_shape=(jax.ShapeDtypeStruct((1, 9, CX, NY, NZ)...  74 us
    unnamed x4, local copies, waits for them, and re-layouts  6.04 us

profile of v1, /device:TPU:9, one launch (start us, length us, event | category | flops | bytes accessed | tf_op | source)
XLA Modules:
  0.0 80.7 jit_solution(15208955143937379644)
XLA Ops:
  0.6 74.0 %shard_map.95 = (f32[1,9,16,64,128]{4,3,2,1,0:T(8,128)}, f32[3,16,16,128]{3,2,1,0:T(8,128)}) custom-call(f32[1,9,16,64,128]{4,3,2,1,0:T(8,128)} %adj.1, f32[1,4,3,16,64,128]{5,4,3,2,1,0:T(8,128)} %fwd.1, f32[16,64,128]{2,1,0:T(8,128)} %vp_h.1, f32[16,64,128]{2,1,0:T(8,128)} %sr_h.1, f32[16,64,128]{2,1,0:T(8,128)} %dn_h.1, f32[3,1,1024]{2,1,0:T(1,128)} %bitcast.3, ...), custom_call_target="tpu_custom_call" | custom-call | tf_op jit(solution)/shard_map/pallas_call | solution.py:533
  74.7 0.0 copy-start
  74.7 5.3 %copy.12 = f32[1,9,16,64,128]{4,3,2,1,0:T(8,128)} copy(f32[1,9,16,64,128]{4,3,2,1,0:T(8,128)} %get-tuple-element.4) | data formatting | bytes 9437184
  80.0 0.0 copy-done
  80.0 0.7 copy.13
Async XLA Ops:
  74.7 5.3 %copy-start = (f32[3,16,16,128]{3,2,1,0:T(8,128)S(1)}, f32[3,16,16,128]{3,2,1,0:T(8,128)}, u32[]{:S(2)}) copy-start(f32[3,16,16,128]{3,2,1,0:T(8,128)} %get-tuple-element.5) | copy-start | bytes 1179652

commit v2 on v1

--- a/solution.py
+++ b/solution.py
@@ -19,7 +19,7 @@
 PAD = 8
 PY = NY + 2 * PAD
 VX, VY, VZ, SXX, SYY, SZZ, SXY, SXZ, SYZ = range(9)
-CHUNKS = (0, 3, 1, 2)
+GROUPS = ((0, 1), (7, 1), (1, 2), (5, 2), (3, 2))
 F32, BF16, I32 = jnp.float32, jnp.bfloat16, jnp.int32
 
 
@@ -42,14 +42,14 @@
 
 
 def kernel(
-    adj, fwd, vp_h, sr_h, dn_h, res, own, cell,
-    out_adj, out_grad,
-    f0, f1, f2, f3, f4, f5, f6, f7, f8,
+    adj, fwd, vp_h, sr_h, dn_h, res_h, own_h, cell_h,
+    f0, f1, f2, f3, f4, f5, f6, f7, f8, h0,
     fw, dense, cb, cl, cm, g0, g1, g2,
-    packed, arrived, a_one, b_one,
-    gs, rb1, s2, rb2, h0, h1, og,
-    load_f, load_w, load_p, out_sem,
-    halo_s, halo_r, fh_s, fh_r, a2a_s, a2a_r,
+    to_left, to_right, from_left, from_right, edge_b, rho_end,
+    res, own, cell, packed, arrived, a_one, b_one,
+    gs, rb1, s2, rb2,
+    load_f, load_w, load_p, load_e, load_c,
+    halo_s, halo_r, eb_s, eb_r, fh_s, fh_r, a2a_s, a2a_r,
     r1_s, r1_r, r2_s, r2_r, gx_s, gx_r,
 ):
     F = (f0, f1, f2, f3, f4, f5, f6, f7, f8)
@@ -66,14 +66,16 @@
     cross = 2 * (1 - chip) + core
     inner = pl.ds(PAD, NY)
 
-    loads_p = [pltpu.make_async_copy(src, dst, load_p.at[i]) for i, (src, dst) in enumerate(((vp_h, cl), (sr_h, cm), (dn_h, cb)))]
-    loads_f = [pltpu.make_async_copy(adj.at[0, k], F[k].at[pl.ds(1, CX), inner], load_f.at[k]) for k in range(9)]
+    ends = ((0, 0), (1, CX - 1))
+    middle = pl.ds(1, CX - 2)
+    loads_e = [pltpu.make_async_copy(dn_h.at[x], cb.at[x], load_e.at[9, i]) for i, x in ends]
+    loads_e += [pltpu.make_async_copy(adj.at[0, k, x], F[k].at[x + 1, inner], load_e.at[k, i]) for k in range(9) for i, x in ends]
+    loads_p = [pltpu.make_async_copy(vp_h, cl, load_p.at[0]), pltpu.make_async_copy(sr_h, cm, load_p.at[1])]
+    loads_p.append(pltpu.make_async_copy(dn_h.at[middle], cb.at[middle], load_p.at[2]))
+    loads_f = [pltpu.make_async_copy(adj.at[0, k, middle], F[k].at[pl.ds(2, CX - 2), inner], load_f.at[k]) for k in range(9)]
     loads_w = [pltpu.make_async_copy(fwd.at[0, t], fw.at[t, :, pl.ds(1, CX), inner], load_w.at[t]) for t in range(STEPS + 1)]
-    for c in loads_p:
-        c.start()
-    for k in (SXX, SXY, SXZ, SYY, SYZ, SZZ, VX, VY, VZ):
-        loads_f[k].start()
-    for c in loads_w:
+    loads_c = [pltpu.make_async_copy(src, dst, load_c.at[i]) for i, (src, dst) in enumerate(((own_h, own), (cell_h, cell), (res_h, res)))]
+    for c in loads_c + loads_e + loads_p + loads_f + loads_w:
         c.start()
 
     zpad = jnp.zeros((PAD, NZ), F32)
@@ -109,16 +111,18 @@
 
     @pl.when(me == 0)
     def _():
-        for k in (VX, SXY, SXZ):
-            F[k][0, inner, :] = zplane
+        edge_b[0] = zplane
         for t in range(STEPS):
             fw[t, 0, 0, inner, :] = zplane
+            for k in range(3):
+                from_left[t, k] = zplane
 
     @pl.when(me == N_SPACE - 1)
     def _():
-        for k in (SXX, VY, VZ):
-            F[k][CX + 1, inner, :] = zplane
+        edge_b[1] = zplane
         for t in range(STEPS):
+            for k in range(3):
+                from_right[t, k] = zplane
             for k in (1, 2):
                 fw[t, k, CX + 1, inner, :] = zplane
 
@@ -132,6 +136,46 @@
     for other in (mate, cross):
         pl.semaphore_signal(barrier, inc=1, device_id={"shot": other}, device_id_type=pl.DeviceIdType.MESH)
 
+    def edges_out(step):
+        for y in range(0, NY, ROWS):
+            def at(k, x, dy=0):
+                return F[k][x, pl.ds(PAD + y + dy, ROWS), :]
+
+            rows = pl.ds(y, ROWS)
+            b = cb[0, rows, :]
+            syz = at(SYZ, 1)
+            to_left[step, 0, rows, :] = at(SXX, 1)
+            to_left[step, 1, rows, :] = at(VY, 1) + b * (at(SXY, 1) + (at(SYY, 1, 1) - at(SYY, 1)) + zminus(syz))
+            to_left[step, 2, rows, :] = at(VZ, 1) + b * (at(SXZ, 1) + (syz - at(SYZ, 1, -1)) + zplus(at(SZZ, 1)))
+            b = cb[CX - 1, rows, :]
+            sxy, sxz = at(SXY, CX), at(SXZ, CX)
+            to_right[step, 0, rows, :] = at(VX, CX) + b * ((sxy - at(SXY, CX, -1)) + zminus(sxz) - at(SXX, CX))
+            to_right[step, 1, rows, :] = sxy
+            to_right[step, 2, rows, :] = sxz
+
+    def edges_in(step):
+        for y in range(0, NY, ROWS):
+            rows = pl.ds(y, ROWS)
+            here = pl.ds(PAD + y, ROWS)
+            b = edge_b[0, rows, :]
+            F[VX][0, here, :] = from_left[step, 0, rows, :] + b * F[SXX][1, here, :]
+            F[SXY][0, here, :] = from_left[step, 1, rows, :]
+            F[SXZ][0, here, :] = from_left[step, 2, rows, :]
+            b = edge_b[1, rows, :]
+            F[SXX][CX + 1, here, :] = from_right[step, 0, rows, :]
+            F[VY][CX + 1, here, :] = from_right[step, 1, rows, :] - b * F[SXY][CX, here, :]
+            F[VZ][CX + 1, here, :] = from_right[step, 2, rows, :] - b * F[SXZ][CX, here, :]
+
+    for c in loads_e:
+        c.wait()
+    for i, x in ends:
+        rho = cb[x]
+        rho_end[i] = rho
+        cb[x] = COURANT * (1.0 / rho)
+    edges_out(0)
+
+    for c in loads_c:
+        c.wait()
     blk = 256
     upper = (lax.broadcasted_iota(I32, (blk, blk), 0) < lax.broadcasted_iota(I32, (blk, blk), 1)).astype(F32).astype(BF16)
     carry_n = jnp.zeros((N_SPACE, 1), F32)
@@ -167,25 +211,17 @@
             src_ref=src, dst_ref=dst, send_sem=s, recv_sem=r, device_id={"space": to}, device_id_type=pl.DeviceIdType.MESH
         )
 
-    def tail_to_right(step, j, k, src=None):
-        src = F[k].at[CX, inner] if src is None else src
-        return send(src, F[k].at[0, inner], halo_s.at[step, j], halo_r.at[step, j], right)
-
-    def head_to_left(step, j, k, src=None):
-        src = F[k].at[1, inner] if src is None else src
-        return send(src, F[k].at[CX + 1, inner], halo_s.at[step, j], halo_r.at[step, j], left)
-
-    def stress_halo(step):
-        hb = step == 0
-        to_left = [head_to_left(step, 0, SXX, adj.at[0, SXX, 0] if hb else None)]
-        to_right = [
-            tail_to_right(step, 1, SXY, adj.at[0, SXY, CX - 1] if hb else None),
-            tail_to_right(step, 2, SXZ, adj.at[0, SXZ, CX - 1] if hb else None),
-        ]
-        return to_left, to_right
-
-    def speed_halo(step):
-        return [head_to_left(step, 3, VY), head_to_left(step, 4, VZ)], [tail_to_right(step, 5, VX)]
+    def edge_halo(step):
+        return (
+            [send(to_left.at[step], from_right.at[step], halo_s.at[step, 0], halo_r.at[step, 0], left)],
+            [send(to_right.at[step], from_left.at[step], halo_s.at[step, 1], halo_r.at[step, 1], right)],
+        )
+
+    def density_halo():
+        return (
+            [send(dn_h.at[0], edge_b.at[1], eb_s.at[0], eb_r.at[0], left)],
+            [send(dn_h.at[CX - 1], edge_b.at[0], eb_s.at[1], eb_r.at[1], right)],
+        )
 
     def forward_halo():
         return (
@@ -226,7 +262,8 @@
             for c in pair[1]:
                 c.wait_send()
 
-    start(stress_halo(0))
+    start(edge_halo(0))
+    start(density_halo())
 
     def channel_copy(k):
         to = (me + k) % N_SPACE
@@ -243,16 +280,22 @@
     for c in loads_p:
         c.wait()
 
-    def params(x, carry):
-        rho, vp, ratio = cb[x], cl[x], cm[x]
+    def lame(x, rho):
+        vp, ratio = cl[x], cm[x]
         vs = ratio * vp
         mu = rho * vs * vs
-        cb[x] = COURANT * (1.0 / rho)
         cl[x] = COURANT * (rho * vp * vp - 2.0 * mu)
         cm[x] = COURANT * mu
-        return carry
-
-    lax.fori_loop(0, CX, params, 0)
+
+    def params(x, carry):
+        rho = cb[x]
+        cb[x] = COURANT * (1.0 / rho)
+        lame(x, rho)
+        return carry
+
+    lax.fori_loop(1, CX - 1, params, 0)
+    for i, x in ends:
+        lame(x, rho_end[i])
     for c in loads_f:
         c.wait()
 
@@ -273,6 +316,7 @@
         return carry
 
     def stresses(step, x, carry=0):
+        inject = step > 0
         for y in range(0, NY, ROWS):
             def at(k, dx=0, dy=0):
                 return F[k][x + dx, pl.ds(PAD + y + dy, ROWS), :]
@@ -288,7 +332,8 @@
             mu2 = mu + mu
             F[SXX][x, here, :] = at(SXX) + (base + mu2 * exx)
             F[SYY][x, here, :] = at(SYY) + (base + mu2 * eyy)
-            F[SZZ][x, here, :] = at(SZZ) + (base + mu2 * ezz)
+            szz = at(SZZ) + (base + mu2 * ezz)
+            F[SZZ][x, here, :] = szz + dense[step, x - 1, flat, :] if inject else szz
             F[SXY][x, here, :] = at(SXY) + mu * ((at(VY, 1) - vy) + (at(VX, 0, 1) - vx))
             F[SXZ][x, here, :] = at(SXZ) + mu * ((at(VZ, 1) - vz) + zplus(vx))
             F[SYZ][x, here, :] = at(SYZ) + mu * ((at(VZ, 0, 1) - vz) + zplus(vy))
@@ -305,11 +350,8 @@
             def w(k):
                 return fw[step + 1, k, x, pl.ds(PAD + y, ROWS), :]
 
-            here = pl.ds(PAD + y, ROWS)
             flat = pl.ds(y, ROWS)
-            sxx, syy = at(SXX), at(SYY)
-            szz = at(SZZ) + dense[step, x - 1, flat, :]
-            F[SZZ][x, here, :] = szz
+            sxx, syy, szz = at(SXX), at(SYY), at(SZZ)
             ux, uy, uz = u(0), u(1), u(2)
             fxx = ux - u(0, -1)
             fyy = uy - u(1, 0, -1)
@@ -359,61 +401,72 @@
 
         lax.fori_loop(0, 4, product, 0)
 
+        def inject(x, carry):
+            F[SZZ][x, inner, :] = F[SZZ][x, inner, :] + dense[0, x - 1]
+            return carry
+
+        lax.fori_loop(1, CX + 1, inject, 0)
+
     for step in range(STEPS):
-        if step > 0:
-            wait_send(speed_halo(step - 1))
         lax.fori_loop(2, CX, speeds, 0)
-        wait_recv(stress_halo(step))
+        lax.fori_loop(3, CX - 1, functools.partial(stresses, step), 0)
+        wait_recv(edge_halo(step))
+        if step == 0:
+            wait_recv(density_halo())
+            for i in range(2):
+                @pl.when(has_left if i == 0 else has_right)
+                def _():
+                    edge_b[i] = COURANT * (1.0 / edge_b[i])
+        edges_in(step)
         speeds(1)
         speeds(CX)
-        start(speed_halo(step))
-        wait_send(stress_halo(step))
-        lax.fori_loop(2, CX, functools.partial(stresses, step), 0)
-        wait_recv(speed_halo(step))
         stresses(step, 1)
         stresses(step, CX)
+        if step == 0:
+            stresses(step, 2)
+            stresses(step, CX - 1)
+            densify()
         if step + 1 < STEPS:
-            start(stress_halo(step + 1))
+            edges_out(step + 1)
+            start(edge_halo(step + 1))
+        if step > 0:
+            stresses(step, 2)
+            stresses(step, CX - 1)
         if step == 0:
-            densify()
             for c in loads_w:
                 c.wait()
             wait_recv(forward_halo())
-        lax.fori_loop(1, CX + 1, functools.partial(gradients, step), 0)
-    wait_send(speed_halo(STEPS - 1))
-    wait_send(forward_halo())
-
-    def channel_sent(k, carry):
-        channel_copy(k).wait_send()
-        return carry
-
-    lax.fori_loop(1, N_SPACE, channel_sent, 0)
-    stores = [pltpu.make_async_copy(F[k].at[pl.ds(1, CX), inner], out_adj.at[0, k], out_sem.at[k]) for k in range(9)]
-    for c in stores:
-        c.start()
-
-    def to_mate(ch):
+        if step + 1 < STEPS:
+            lax.fori_loop(1, CX + 1, functools.partial(gradients, step), 0)
+
+    def to_mate(n):
+        pairs = pl.ds(*GROUPS[n])
         return [
             pltpu.make_async_remote_copy(
-                src_ref=gs.at[2 * j + 1 - core, :, pl.ds(2 * ch, 2)],
-                dst_ref=rb1.at[j, :, pl.ds(2 * ch, 2)],
-                send_sem=r1_s.at[ch, j],
-                recv_sem=r1_r.at[ch, j],
+                src_ref=gs.at[2 * j + 1 - core, :, pairs],
+                dst_ref=rb1.at[j, :, pairs],
+                send_sem=r1_s.at[n, j],
+                recv_sem=r1_r.at[n, j],
                 device_id={"shot": mate},
                 device_id_type=pl.DeviceIdType.MESH,
             )
             for j in range(2)
         ]
 
-    def to_cross(ch):
+    def to_cross(n):
+        pairs = pl.ds(*GROUPS[n])
         return pltpu.make_async_remote_copy(
-            src_ref=s2.at[:, pl.ds(2 * ch, 2)],
-            dst_ref=rb2.at[:, pl.ds(2 * ch, 2)],
-            send_sem=r2_s.at[ch],
-            recv_sem=r2_r.at[ch],
+            src_ref=s2.at[:, pairs],
+            dst_ref=rb2.at[:, pairs],
+            send_sem=r2_s.at[n],
+            recv_sem=r2_r.at[n],
             device_id={"shot": cross},
             device_id_type=pl.DeviceIdType.MESH,
         )
+
+    def pairs_of(n, body):
+        first, count = GROUPS[n]
+        lax.fori_loop(first, first + count, body, 0)
 
     def slabs(i, carry):
         for k in range(3):
@@ -424,21 +477,25 @@
                     gs[s, k, i, pl.ds(off, hi - lo), :] = G[k][2 * i + xx, pl.ds(lo, hi - lo), :]
         return carry
 
-    for ch in CHUNKS:
-        lax.fori_loop(2 * ch, 2 * ch + 2, slabs, 0)
-        for c in to_mate(ch):
-            c.start()
-
     def sum_cross(i, carry):
         for k in range(3):
             s2[k, i] = gs[2 * (1 - chip) + core, k, i] + rb1[1 - chip, k, i]
         return carry
 
-    for ch in CHUNKS:
-        for c in to_mate(ch):
+    def pass_on(n):
+        for c in to_mate(n):
             c.wait_recv()
-        lax.fori_loop(2 * ch, 2 * ch + 2, sum_cross, 0)
-        to_cross(ch).start()
+        pairs_of(n, sum_cross)
+        to_cross(n).start()
+
+    for n, (first, count) in enumerate(GROUPS):
+        lax.fori_loop(2 * first + 1, 2 * (first + count) + 1, functools.partial(gradients, STEPS - 1), 0)
+        pairs_of(n, slabs)
+        for c in to_mate(n):
+            c.start()
+        if n > 0:
+            pass_on(n - 1)
+    pass_on(len(GROUPS) - 1)
 
     def sum_own(i, carry):
         for k in range(3):
@@ -453,13 +510,37 @@
         [send(h0.at[:, pl.ds(2, 2), rim], h0.at[:, pl.ds(CX + 2, 2), rim], gx_s.at[0], gx_r.at[0], left)],
         [send(h0.at[:, pl.ds(CX, 2), rim], h0.at[:, pl.ds(0, 2), rim], gx_s.at[1], gx_r.at[1], right)],
     )
-    for n, ch in enumerate(CHUNKS):
-        to_cross(ch).wait_recv()
-        lax.fori_loop(2 * ch, 2 * ch + 2, sum_own, 0)
+    for n in range(len(GROUPS)):
+        to_cross(n).wait_recv()
+        pairs_of(n, sum_own)
         if n == 1:
             start(grad_halo)
     wait_recv(grad_halo)
     wait_send(grad_halo)
+
+    for step in range(STEPS):
+        wait_send(edge_halo(step))
+    wait_send(density_halo())
+    wait_send(forward_halo())
+
+    def channel_sent(k, carry):
+        channel_copy(k).wait_send()
+        return carry
+
+    lax.fori_loop(1, N_SPACE, channel_sent, 0)
+    for n in range(len(GROUPS)):
+        for c in to_mate(n):
+            c.wait_send()
+        to_cross(n).wait_send()
+
+
+def finish(f0, f1, f2, f3, f4, f5, f6, f7, f8, h0, out_adj, out_grad, h1, og, sem):
+    me = lax.axis_index("space")
+    sh = lax.axis_index("shot")
+    fields = (f0, f1, f2, f3, f4, f5, f6, f7, f8)
+    stores = [pltpu.make_async_copy(f.at[pl.ds(1, CX), pl.ds(PAD, NY)], out_adj.at[0, k], sem.at[k]) for k, f in enumerate(fields)]
+    for c in stores:
+        c.start()
 
     def near(h, k, p, lo, n):
         def at(dp=0, dy=0):
@@ -476,7 +557,7 @@
         gy = 16 * sh - 2 + lax.broadcasted_iota(I32, (24, NZ), 0)
         keep = (gy >= 0) & (gy < NY) & (gx >= 0) & (gx < NX)
         for k in range(3):
-            h1[k, p, rim, :] = jnp.where(keep, near(h0, k, p, 8, 24), 0.0)
+            h1[k, p, pl.ds(8, 24), :] = jnp.where(keep, near(h0, k, p, 8, 24), 0.0)
         return carry
 
     lax.fori_loop(1, CX + 3, sweep_one, 0)
@@ -487,33 +568,36 @@
         return carry
 
     lax.fori_loop(0, CX, sweep_two, 0)
-    grad_out = pltpu.make_async_copy(og, out_grad, out_sem.at[9])
+    grad_out = pltpu.make_async_copy(og, out_grad, sem.at[9])
     grad_out.start()
-    for ch in CHUNKS:
-        for c in to_mate(ch):
-            c.wait_send()
-        to_cross(ch).wait_send()
+    grad_out.wait()
     for c in stores:
         c.wait()
-    grad_out.wait()
 
 
 def local(adjoint_state, forward_velocity, vp, shear_ratio, density, residuals, owner, cell):
     res = residuals.reshape(STEPS, 1, CH_DEV)
     own = owner.reshape(1, CH_DEV)
     cells = cell.reshape(1, CH_DEV)
-    hbm = pl.BlockSpec(memory_space=pl.ANY)
+    hbm = pl.BlockSpec(memory_space=pltpu.HBM)
     vmem = pl.BlockSpec(memory_space=pltpu.VMEM)
     volume = pltpu.VMEM((CX, NY, NZ), F32)
     dma = pltpu.SemaphoreType.DMA
+    edges = pltpu.VMEM((STEPS, 3, NY, NZ), F32)
+    pair = pltpu.VMEM((2, NY, NZ), F32)
+    count = len(GROUPS)
     scratch = (
-        [pltpu.VMEM((CX + 2, PY, NZ), F32)] * 9
-        + [
+        [
             pltpu.VMEM((STEPS + 1, 3, CX + 2, PY, NZ), F32),
             pltpu.VMEM((STEPS, CX, NY, NZ), F32),
         ]
         + [volume] * 6
+        + [edges] * 4
+        + [pair] * 2
         + [
+            pltpu.VMEM((STEPS, 1, CH_DEV), F32),
+            pltpu.VMEM((1, CH_DEV), I32),
+            pltpu.VMEM((1, CH_DEV), I32),
             pltpu.VMEM((N_SPACE, 8, CAP), F32),
             pltpu.VMEM((N_SPACE, 8, CAP), F32),
             pltpu.VMEM((CX * NY, N_SPACE * CAP), BF16),
@@ -522,25 +606,34 @@
             pltpu.VMEM((2, 3, CX // 2, 40, NZ), F32),
             pltpu.VMEM((3, CX // 2, 40, NZ), F32),
             pltpu.VMEM((3, CX // 2, 40, NZ), F32),
-            pltpu.VMEM((3, CX + 4, 40, NZ), F32),
-            pltpu.VMEM((3, CX + 4, 40, NZ), F32),
-            pltpu.VMEM((3, CX, 16, NZ), F32),
         ]
-        + [dma((9,)), dma((4,)), dma((3,)), dma((10,))]
-        + [dma((STEPS, 6)), dma((STEPS, 6)), dma((2,)), dma((2,)), dma((N_SPACE,)), dma((N_SPACE,))]
-        + [dma((4, 2)), dma((4, 2)), dma((4,)), dma((4,)), dma((2,)), dma((2,))]
+        + [dma((9,)), dma((4,)), dma((3,)), dma((10, 2)), dma((3,))]
+        + [dma((STEPS, 2)), dma((STEPS, 2)), dma((2,)), dma((2,)), dma((2,)), dma((2,)), dma((N_SPACE,)), dma((N_SPACE,))]
+        + [dma((count, 2)), dma((count, 2)), dma((count,)), dma((count,)), dma((2,)), dma((2,))]
     )
+    held = [(CX + 2, PY, NZ)] * 9 + [(3, CX + 4, 40, NZ)]
+    given = (adjoint_state, forward_velocity, vp, shear_ratio, density, res, own, cells)
+    given = [pltpu.with_memory_space_constraint(a, pltpu.HBM) for a in given]
+    kept = pl.pallas_call(
+        kernel,
+        out_shape=tuple(pltpu.VMEM(shape, F32) for shape in held),
+        in_specs=[hbm] * 8,
+        out_specs=(vmem,) * len(held),
+        scratch_shapes=scratch,
+        compiler_params=pltpu.CompilerParams(collective_id=0, has_side_effects=True, vmem_limit_bytes=44 * 1024 * 1024),
+    )(*given)
+    kept = [pltpu.with_memory_space_constraint(a, pltpu.VMEM) for a in kept]
     return pl.pallas_call(
-        kernel,
+        finish,
         out_shape=(
             jax.ShapeDtypeStruct((1, 9, CX, NY, NZ), F32),
             jax.ShapeDtypeStruct((3, CX, 16, NZ), F32),
         ),
-        in_specs=[hbm] * 5 + [vmem] * 3,
+        in_specs=[vmem] * len(held),
         out_specs=(hbm, hbm),
-        scratch_shapes=scratch,
-        compiler_params=pltpu.CompilerParams(collective_id=0, has_side_effects=True, vmem_limit_bytes=60 * 1024 * 1024),
-    )(adjoint_state, forward_velocity, vp, shear_ratio, density, res, own, cells)
+        scratch_shapes=[pltpu.VMEM((3, CX + 4, 40, NZ), F32), pltpu.VMEM((3, CX, 16, NZ), F32), dma((10,))],
+        compiler_params=pltpu.CompilerParams(vmem_limit_bytes=8 * 1024 * 1024),
+    )(*kept)
 
 
 def solution(mesh):

time: 80.9 us -> 62.8 us (0.78)
  Pallas kernels: 74 us -> 62 us
  local copies, waits for them, and re-layouts: 6.04 us -> 0 us
    pallas_call x1 -> x2, Pallas kernels: 74 us -> 62 us  [the longest x1 58.1 us: local(): pl.pallas_call(kernel, out_shape=tuple((pltpu.VMEM(shape, F32) for shape...]
    unnamed x4 -> x0, local copies, waits for them, and re-layouts: 6.04 us -> none
where the time goes in v2:
time: 62.8 us; the launch traced here: 62.7 us
  Pallas kernels  62 us (99%)
  between operations  0.64 us (1%)
    pallas_call x1, Pallas kernels, local(): pl.pallas_call(kernel, out_shape=tuple((pltpu.VMEM(shape, F32) for shape...  58.1 us
    pallas_call x1, Pallas kernels, local(): pl.pallas_call(finish, out_shape=(jax.ShapeDtypeStruct((1, 9, CX, NY, NZ)...  3.88 us

profile of v2, /device:TPU:9, one launch (start us, length us, event | category | flops | bytes accessed | tf_op | source)
XLA Modules:
  0.0 62.7 jit_solution(18117773890961441991)
XLA Ops:
  0.6 58.1 %shard_map.95 = (f32[18,80,128]{2,1,0:T(8,128)S(1)}, f32[18,80,128]{2,1,0:T(8,128)S(1)}, f32[18,80,128]{2,1,0:T(8,128)S(1)}, f32[18,80,128]{2,1,0:T(8,128)S(1)},...) custom-call(f32[1,9,16,64,128]{4,3,2,1,0:T(8,128)} %adj.1, ...), custom_call_target="tpu_custom_call" | custom-call | tf_op jit(solution)/shard_map/pallas_call | solution.py:617
  58.8 3.9 %shard_map.96 = (f32[1,9,16,64,128]{4,3,2,1,0:T(8,128)}, f32[3,16,16,128]{3,2,1,0:T(8,128)}) custom-call(f32[18,80,128]{2,1,0:T(8,128)S(1)} %get-tuple-element.12.f0, f32[18,80,128]{2,1,0:T(8,128)S(1)} %get-tuple-element.13.f1, f32[18,80,128]{2,1,0:T(8,128)S(1)} %get-tuple-element.14.f2, f32[18,80,128]{2,1,0:T(8,128)S(1)} %get-tuple-element.15.f3, ...), custom_call_target="tpu_custom_call" | custom-call | tf_op jit(solution)/shard_map/pallas_call | solution.py:626

commit v3 on v2

--- a/solution.py
+++ b/solution.py
@@ -19,7 +19,7 @@
 PAD = 8
 PY = NY + 2 * PAD
 VX, VY, VZ, SXX, SYY, SZZ, SXY, SXZ, SYZ = range(9)
-GROUPS = ((0, 1), (7, 1), (1, 2), (5, 2), (3, 2))
+GROUPS = ((3, 1), (0, 1), (7, 1), (1, 2), (5, 2), (4, 1))
 F32, BF16, I32 = jnp.float32, jnp.bfloat16, jnp.int32
 
 
@@ -376,68 +376,85 @@
         lax.fori_loop(1, N_SPACE, channel_wait, 0)
 
         def one_hot(s, carry):
-            lanes = pl.ds(pl.multiple_of(s * CAP, CAP), CAP)
             row = arrived[s]
             x, y, z = row[3:4].astype(I32), row[4:5].astype(I32), row[5:6].astype(I32)
-            yone = (y == lax.broadcasted_iota(I32, (NY, CAP), 0)).astype(F32)
-            zone = (z == lax.broadcasted_iota(I32, (NZ, CAP), 0)).astype(F32)
+
+            def tile(v):
+                return jnp.broadcast_to(v, (16, CAP)).astype(BF16)
+
+            yone = (y == lax.broadcasted_iota(I32, (NY, CAP), 0)).astype(F32).astype(BF16)
+            zone = (z == lax.broadcasted_iota(I32, (NZ, CAP), 0)).astype(F32).astype(BF16)
+            yone, zone = yone.reshape(NY // 16, 16, CAP), zone.reshape(NZ // 16, 16, CAP)
             for i in range(CX):
-                a_one[pl.ds(i * NY, NY), lanes] = jnp.where(x == i, yone, 0.0).astype(BF16)
+                xone = tile((x == i).astype(F32))
+                a_one[s, pl.ds(i * NY, NY), :] = (yone * xone[None]).reshape(NY, CAP)
             for t in range(STEPS):
                 v = row[t : t + 1]
                 hi = v.astype(BF16).astype(F32)
-                b_one[pl.ds(2 * t * NZ, NZ), lanes] = (zone * hi).astype(BF16)
-                b_one[pl.ds((2 * t + 1) * NZ, NZ), lanes] = (zone * (v - hi)).astype(BF16)
+                b_one[t, s, pl.ds(0, NZ), :] = (zone * tile(hi)[None]).reshape(NZ, CAP)
+                b_one[t, s, pl.ds(NZ, NZ), :] = (zone * tile(v - hi)[None]).reshape(NZ, CAP)
             return carry
 
         lax.fori_loop(0, N_SPACE, one_hot, 0)
 
-        def product(m, carry):
-            got = nt(a_one[pl.ds(pl.multiple_of(m * 256, 256), 256), :], b_one[...])
-            for t in range(STEPS):
-                both = got[:, 2 * t * NZ : (2 * t + 1) * NZ] + got[:, (2 * t + 1) * NZ : (2 * t + 2) * NZ]
-                dense[t, pl.ds(4 * m, 4), :, :] = both.reshape(4, NY, NZ)
-            return carry
-
-        lax.fori_loop(0, 4, product, 0)
-
-        def inject(x, carry):
+    def product(m, t):
+        rows = pl.ds(pl.multiple_of(m * 256, 256), 256)
+        got = nt(
+            jnp.concatenate([a_one[s, rows, :] for s in range(N_SPACE)], axis=1),
+            jnp.concatenate([b_one[t, s] for s in range(N_SPACE)], axis=1),
+        )
+        dense[t, pl.ds(4 * m, 4), :, :] = (got[:, :NZ] + got[:, NZ:]).reshape(4, NY, NZ)
+
+    def first_product(m, carry):
+        product(m, 0)
+        for i in range(4):
+            x = 4 * m + i + 1
             F[SZZ][x, inner, :] = F[SZZ][x, inner, :] + dense[0, x - 1]
-            return carry
-
-        lax.fori_loop(1, CX + 1, inject, 0)
-
-    for step in range(STEPS):
-        lax.fori_loop(2, CX, speeds, 0)
-        lax.fori_loop(3, CX - 1, functools.partial(stresses, step), 0)
-        wait_recv(edge_halo(step))
-        if step == 0:
-            wait_recv(density_halo())
-            for i in range(2):
-                @pl.when(has_left if i == 0 else has_right)
-                def _():
-                    edge_b[i] = COURANT * (1.0 / edge_b[i])
+        return carry
+
+    def later_products(m, carry):
+        for t in range(1, STEPS):
+            product(m, t)
+        for i in range(4):
+            gradients(0, 4 * m + i + 1)
+        return carry
+
+    def end_planes(step):
         edges_in(step)
         speeds(1)
         speeds(CX)
-        stresses(step, 1)
-        stresses(step, CX)
-        if step == 0:
-            stresses(step, 2)
-            stresses(step, CX - 1)
-            densify()
-        if step + 1 < STEPS:
-            edges_out(step + 1)
-            start(edge_halo(step + 1))
-        if step > 0:
-            stresses(step, 2)
-            stresses(step, CX - 1)
-        if step == 0:
-            for c in loads_w:
-                c.wait()
-            wait_recv(forward_halo())
-        if step + 1 < STEPS:
-            lax.fori_loop(1, CX + 1, functools.partial(gradients, step), 0)
+
+    lax.fori_loop(2, CX, speeds, 0)
+    lax.fori_loop(3, CX - 1, functools.partial(stresses, 0), 0)
+    wait_recv(edge_halo(0))
+    wait_recv(density_halo())
+    for i in range(2):
+        @pl.when(has_left if i == 0 else has_right)
+        def _():
+            edge_b[i] = COURANT * (1.0 / edge_b[i])
+    end_planes(0)
+    for x in (1, 2, CX - 1, CX):
+        stresses(0, x)
+    densify()
+    lax.fori_loop(0, 4, first_product, 0)
+    edges_out(1)
+    start(edge_halo(1))
+    for c in loads_w:
+        c.wait()
+    wait_recv(forward_halo())
+    lax.fori_loop(0, 4, later_products, 0)
+
+    lax.fori_loop(2, CX, speeds, 0)
+    wait_recv(edge_halo(1))
+    end_planes(1)
+    stresses(1, 1)
+    stresses(1, CX)
+    edges_out(2)
+    start(edge_halo(2))
+    lax.fori_loop(2, CX, functools.partial(stresses, 1), 0)
+    lax.fori_loop(1, CX + 1, functools.partial(gradients, 1), 0)
+
+    lax.fori_loop(2, CX, speeds, 0)
 
     def to_mate(n):
         pairs = pl.ds(*GROUPS[n])
@@ -488,8 +505,16 @@
         pairs_of(n, sum_cross)
         to_cross(n).start()
 
+    def last(x, carry):
+        stresses(STEPS - 1, x)
+        gradients(STEPS - 1, x)
+        return carry
+
     for n, (first, count) in enumerate(GROUPS):
-        lax.fori_loop(2 * first + 1, 2 * (first + count) + 1, functools.partial(gradients, STEPS - 1), 0)
+        if n == 1:
+            wait_recv(edge_halo(2))
+            end_planes(2)
+        lax.fori_loop(2 * first + 1, 2 * (first + count) + 1, last, 0)
         pairs_of(n, slabs)
         for c in to_mate(n):
             c.start()
@@ -513,7 +538,7 @@
     for n in range(len(GROUPS)):
         to_cross(n).wait_recv()
         pairs_of(n, sum_own)
-        if n == 1:
+        if n == 2:
             start(grad_halo)
     wait_recv(grad_halo)
     wait_send(grad_halo)
@@ -600,8 +625,8 @@
             pltpu.VMEM((1, CH_DEV), I32),
             pltpu.VMEM((N_SPACE, 8, CAP), F32),
             pltpu.VMEM((N_SPACE, 8, CAP), F32),
-            pltpu.VMEM((CX * NY, N_SPACE * CAP), BF16),
-            pltpu.VMEM((2 * STEPS * NZ, N_SPACE * CAP), BF16),
+            pltpu.VMEM((N_SPACE, CX * NY, CAP), BF16),
+            pltpu.VMEM((STEPS, N_SPACE, 2 * NZ, CAP), BF16),
             pltpu.VMEM((4, 3, CX // 2, 40, NZ), F32),
             pltpu.VMEM((2, 3, CX // 2, 40, NZ), F32),
             pltpu.VMEM((3, CX // 2, 40, NZ), F32),

time: 62.8 us -> 57.7 us (0.919)
  Pallas kernels: 62 us -> 57 us
    pallas_call x1, Pallas kernels: 58.1 us -> 53.1 us  [local(): pl.pallas_call(kernel, out_shape=tuple((pltpu.VMEM(shape, F32) for shape...]
where the time goes in v3:
time: 57.7 us; the launch traced here: 57.6 us
  Pallas kernels  57 us (99%)
  between operations  0.64 us (1%)
    pallas_call x1, Pallas kernels, local(): pl.pallas_call(kernel, out_shape=tuple((pltpu.VMEM(shape, F32) for shape...  53.1 us
    pallas_call x1, Pallas kernels, local(): pl.pallas_call(finish, out_shape=(jax.ShapeDtypeStruct((1, 9, CX, NY, NZ)...  3.88 us

profile of v3, /device:TPU:9, one launch (start us, length us, event | category | flops | bytes accessed | tf_op | source)
XLA Modules:
  0.0 57.6 jit_solution(8071832182539466653)
XLA Ops:
  0.6 53.1 %shard_map.95 = (f32[18,80,128]{2,1,0:T(8,128)S(1)}, f32[18,80,128]{2,1,0:T(8,128)S(1)}, f32[18,80,128]{2,1,0:T(8,128)S(1)}, f32[18,80,128]{2,1,0:T(8,128)S(1)},...) custom-call(f32[1,9,16,64,128]{4,3,2,1,0:T(8,128)} %adj.1, ...), custom_call_target="tpu_custom_call" | custom-call | tf_op jit(solution)/shard_map/pallas_call | solution.py:642
  53.8 3.9 %shard_map.96 = (f32[1,9,16,64,128]{4,3,2,1,0:T(8,128)}, f32[3,16,16,128]{3,2,1,0:T(8,128)}) custom-call(f32[18,80,128]{2,1,0:T(8,128)S(1)} %get-tuple-element.12.f0, f32[18,80,128]{2,1,0:T(8,128)S(1)} %get-tuple-element.13.f1, f32[18,80,128]{2,1,0:T(8,128)S(1)} %get-tuple-element.14.f2, f32[18,80,128]{2,1,0:T(8,128)S(1)} %get-tuple-element.15.f3, ...), custom_call_target="tpu_custom_call" | custom-call | tf_op jit(solution)/shard_map/pallas_call | solution.py:651

commit v4 on v3

--- a/solution.py
+++ b/solution.py
@@ -19,7 +19,7 @@
 PAD = 8
 PY = NY + 2 * PAD
 VX, VY, VZ, SXX, SYY, SZZ, SXY, SXZ, SYZ = range(9)
-GROUPS = ((3, 1), (0, 1), (7, 1), (1, 2), (5, 2), (4, 1))
+GROUPS = ((3, 2), (0, 1), (7, 1), (1, 2), (5, 2))
 F32, BF16, I32 = jnp.float32, jnp.bfloat16, jnp.int32
 
 
@@ -75,8 +75,18 @@
     loads_f = [pltpu.make_async_copy(adj.at[0, k, middle], F[k].at[pl.ds(2, CX - 2), inner], load_f.at[k]) for k in range(9)]
     loads_w = [pltpu.make_async_copy(fwd.at[0, t], fw.at[t, :, pl.ds(1, CX), inner], load_w.at[t]) for t in range(STEPS + 1)]
     loads_c = [pltpu.make_async_copy(src, dst, load_c.at[i]) for i, (src, dst) in enumerate(((own_h, own), (cell_h, cell), (res_h, res)))]
-    for c in loads_c + loads_e + loads_p + loads_f + loads_w:
+    for c in loads_e + loads_c + loads_f + loads_p + loads_w:
         c.start()
+
+    barrier = pltpu.get_barrier_semaphore()
+
+    def greet(k, carry):
+        pl.semaphore_signal(barrier, inc=1, device_id={"space": (me + k) % N_SPACE}, device_id_type=pl.DeviceIdType.MESH)
+        return carry
+
+    for other in (mate, cross):
+        pl.semaphore_signal(barrier, inc=1, device_id={"shot": other}, device_id_type=pl.DeviceIdType.MESH)
+    lax.fori_loop(1, N_SPACE, greet, 0)
 
     zpad = jnp.zeros((PAD, NZ), F32)
 
@@ -90,23 +100,8 @@
                 fw[t, k, x, pl.ds(PAD + NY, PAD), :] = zpad
         return carry
 
-    lax.fori_loop(1, CX + 1, zero_pads, 0)
-
-    def zero_h(x, carry):
-        for k in range(3):
-            h0[k, x, :, :] = jnp.zeros((40, NZ), F32)
-        return carry
-
-    lax.fori_loop(0, CX + 4, zero_h, 0)
-
-    def zero_gs(i, carry):
-        for k in range(3):
-            for xx in range(2):
-                gs[0, k, i, pl.ds(20 * xx, 2), :] = jnp.zeros((2, NZ), F32)
-                gs[3, k, i, pl.ds(20 * xx + 18, 2), :] = jnp.zeros((2, NZ), F32)
-        return carry
-
-    lax.fori_loop(0, CX // 2, zero_gs, 0)
+    zero_pads(1, 0)
+    zero_pads(CX, 0)
     zplane = jnp.zeros((NY, NZ), F32)
 
     @pl.when(me == 0)
@@ -125,16 +120,6 @@
                 from_right[t, k] = zplane
             for k in (1, 2):
                 fw[t, k, CX + 1, inner, :] = zplane
-
-    barrier = pltpu.get_barrier_semaphore()
-
-    def greet(k, carry):
-        pl.semaphore_signal(barrier, inc=1, device_id={"space": (me + k) % N_SPACE}, device_id_type=pl.DeviceIdType.MESH)
-        return carry
-
-    lax.fori_loop(1, N_SPACE, greet, 0)
-    for other in (mate, cross):
-        pl.semaphore_signal(barrier, inc=1, device_id={"shot": other}, device_id_type=pl.DeviceIdType.MESH)
 
     def edges_out(step):
         for y in range(0, NY, ROWS):
@@ -173,6 +158,67 @@
         rho_end[i] = rho
         cb[x] = COURANT * (1.0 / rho)
     edges_out(0)
+
+    pl.semaphore_wait(barrier, N_SPACE + 1)
+
+    def send(src, dst, s, r, to):
+        return pltpu.make_async_remote_copy(
+            src_ref=src, dst_ref=dst, send_sem=s, recv_sem=r, device_id={"space": to}, device_id_type=pl.DeviceIdType.MESH
+        )
+
+    def edge_halo(step):
+        return (
+            [send(to_left.at[step], from_right.at[step], halo_s.at[step, 0], halo_r.at[step, 0], left)],
+            [send(to_right.at[step], from_left.at[step], halo_s.at[step, 1], halo_r.at[step, 1], right)],
+        )
+
+    def density_halo():
+        return (
+            [send(dn_h.at[0], edge_b.at[1], eb_s.at[0], eb_r.at[0], left)],
+            [send(dn_h.at[CX - 1], edge_b.at[0], eb_s.at[1], eb_r.at[1], right)],
+        )
+
+    def forward_halo():
+        return (
+            [send(fwd.at[0, pl.ds(0, STEPS), pl.ds(1, 2), 0], fw.at[pl.ds(0, STEPS), pl.ds(1, 2), CX + 1, inner], fh_s.at[0], fh_r.at[0], left)],
+            [send(fwd.at[0, pl.ds(0, STEPS), 0, CX - 1], fw.at[pl.ds(0, STEPS), 0, 0, inner], fh_s.at[1], fh_r.at[1], right)],
+        )
+
+    def start(pair):
+        @pl.when(has_left)
+        def _():
+            for c in pair[0]:
+                c.start()
+
+        @pl.when(has_right)
+        def _():
+            for c in pair[1]:
+                c.start()
+
+    def wait_recv(pair):
+        @pl.when(has_right)
+        def _():
+            for c in pair[0]:
+                c.wait_recv()
+
+        @pl.when(has_left)
+        def _():
+            for c in pair[1]:
+                c.wait_recv()
+
+    def wait_send(pair):
+        @pl.when(has_left)
+        def _():
+            for c in pair[0]:
+                c.wait_send()
+
+        @pl.when(has_right)
+        def _():
+            for c in pair[1]:
+                c.wait_send()
+
+    start(edge_halo(0))
+    start(density_halo())
 
     for c in loads_c:
         c.wait()
@@ -204,67 +250,6 @@
     acc = acc.reshape(N_SPACE, 16, CAP)
     packed[...] = acc[:, :8, :] + acc[:, 8:, :]
 
-    pl.semaphore_wait(barrier, N_SPACE + 1)
-
-    def send(src, dst, s, r, to):
-        return pltpu.make_async_remote_copy(
-            src_ref=src, dst_ref=dst, send_sem=s, recv_sem=r, device_id={"space": to}, device_id_type=pl.DeviceIdType.MESH
-        )
-
-    def edge_halo(step):
-        return (
-            [send(to_left.at[step], from_right.at[step], halo_s.at[step, 0], halo_r.at[step, 0], left)],
-            [send(to_right.at[step], from_left.at[step], halo_s.at[step, 1], halo_r.at[step, 1], right)],
-        )
-
-    def density_halo():
-        return (
-            [send(dn_h.at[0], edge_b.at[1], eb_s.at[0], eb_r.at[0], left)],
-            [send(dn_h.at[CX - 1], edge_b.at[0], eb_s.at[1], eb_r.at[1], right)],
-        )
-
-    def forward_halo():
-        return (
-            [send(fwd.at[0, pl.ds(0, STEPS), pl.ds(1, 2), 0], fw.at[pl.ds(0, STEPS), pl.ds(1, 2), CX + 1, inner], fh_s.at[0], fh_r.at[0], left)],
-            [send(fwd.at[0, pl.ds(0, STEPS), 0, CX - 1], fw.at[pl.ds(0, STEPS), 0, 0, inner], fh_s.at[1], fh_r.at[1], right)],
-        )
-
-    def start(pair):
-        @pl.when(has_left)
-        def _():
-            for c in pair[0]:
-                c.start()
-
-        @pl.when(has_right)
-        def _():
-            for c in pair[1]:
-                c.start()
-
-    def wait_recv(pair):
-        @pl.when(has_right)
-        def _():
-            for c in pair[0]:
-                c.wait_recv()
-
-        @pl.when(has_left)
-        def _():
-            for c in pair[1]:
-                c.wait_recv()
-
-    def wait_send(pair):
-        @pl.when(has_left)
-        def _():
-            for c in pair[0]:
-                c.wait_send()
-
-        @pl.when(has_right)
-        def _():
-            for c in pair[1]:
-                c.wait_send()
-
-    start(edge_halo(0))
-    start(density_halo())
-
     def channel_copy(k):
         to = (me + k) % N_SPACE
         return send(packed.at[to], arrived.at[me], a2a_s.at[k], a2a_r.at[k], to)
@@ -276,6 +261,24 @@
     lax.fori_loop(1, N_SPACE, channel_start, 0)
     start(forward_halo())
     arrived[me] = packed[me]
+
+    lax.fori_loop(2, CX, zero_pads, 0)
+
+    def zero_h(x, carry):
+        for k in range(3):
+            h0[k, x, :, :] = jnp.zeros((40, NZ), F32)
+        return carry
+
+    lax.fori_loop(0, CX + 4, zero_h, 0)
+
+    def zero_gs(i, carry):
+        for k in range(3):
+            for xx in range(2):
+                gs[0, k, i, pl.ds(20 * xx, 2), :] = jnp.zeros((2, NZ), F32)
+                gs[3, k, i, pl.ds(20 * xx + 18, 2), :] = jnp.zeros((2, NZ), F32)
+        return carry
+
+    lax.fori_loop(0, CX // 2, zero_gs, 0)
 
     for c in loads_p:
         c.wait()
@@ -315,8 +318,7 @@
             F[VZ][x, here, :] = vz
         return carry
 
-    def stresses(step, x, carry=0):
-        inject = step > 0
+    def stresses(step, x, carry=0, add=False):
         for y in range(0, NY, ROWS):
             def at(k, dx=0, dy=0):
                 return F[k][x + dx, pl.ds(PAD + y + dy, ROWS), :]
@@ -330,42 +332,47 @@
             ezz = zminus(vz)
             base = lam * (exx + eyy + ezz)
             mu2 = mu + mu
-            F[SXX][x, here, :] = at(SXX) + (base + mu2 * exx)
-            F[SYY][x, here, :] = at(SYY) + (base + mu2 * eyy)
             szz = at(SZZ) + (base + mu2 * ezz)
-            F[SZZ][x, here, :] = szz + dense[step, x - 1, flat, :] if inject else szz
-            F[SXY][x, here, :] = at(SXY) + mu * ((at(VY, 1) - vy) + (at(VX, 0, 1) - vx))
-            F[SXZ][x, here, :] = at(SXZ) + mu * ((at(VZ, 1) - vz) + zplus(vx))
-            F[SYZ][x, here, :] = at(SYZ) + mu * ((at(VZ, 0, 1) - vz) + zplus(vy))
-        return carry
+            new = [
+                at(SXX) + (base + mu2 * exx),
+                at(SYY) + (base + mu2 * eyy),
+                szz + dense[step, x - 1, flat, :] if step > 0 else szz,
+                at(SXY) + mu * ((at(VY, 1) - vy) + (at(VX, 0, 1) - vx)),
+                at(SXZ) + mu * ((at(VZ, 1) - vz) + zplus(vx)),
+                at(SYZ) + mu * ((at(VZ, 0, 1) - vz) + zplus(vy)),
+            ]
+            for k, v in zip((SXX, SYY, SZZ, SXY, SXZ, SYZ), new):
+                F[k][x, here, :] = v
+            if add:
+                add_terms(step, x, y, vx, vy, vz, *new)
+        return carry
+
+    def add_terms(step, x, y, vx, vy, vz, sxx, syy, szz, sxy, sxz, syz):
+        def u(k, dx=0, dy=0):
+            return fw[step, k, x + dx, pl.ds(PAD + y + dy, ROWS), :]
+
+        def w(k):
+            return fw[step + 1, k, x, pl.ds(PAD + y, ROWS), :]
+
+        flat = pl.ds(y, ROWS)
+        ux, uy, uz = u(0), u(1), u(2)
+        fxx = ux - u(0, -1)
+        fyy = uy - u(1, 0, -1)
+        fzz = zminus(uz)
+        lam = (fxx + fyy + fzz) * (sxx + syy + szz)
+        mu = (
+            2.0 * (fxx * sxx + fyy * syy + fzz * szz)
+            + ((u(1, 1) - uy) + (u(0, 0, 1) - ux)) * sxy
+            + ((u(2, 1) - uz) + zplus(ux)) * sxz
+            + ((u(2, 0, 1) - uz) + zplus(uy)) * syz
+        )
+        rho = vx * (w(0) - ux) + vy * (w(1) - uy) + vz * (w(2) - uz)
+        for ref, term in zip(G, (lam, mu, rho)):
+            ref[x - 1, flat, :] = term if step == 0 else ref[x - 1, flat, :] + term
 
     def gradients(step, x, carry=0):
         for y in range(0, NY, ROWS):
-            def at(k):
-                return F[k][x, pl.ds(PAD + y, ROWS), :]
-
-            def u(k, dx=0, dy=0):
-                return fw[step, k, x + dx, pl.ds(PAD + y + dy, ROWS), :]
-
-            def w(k):
-                return fw[step + 1, k, x, pl.ds(PAD + y, ROWS), :]
-
-            flat = pl.ds(y, ROWS)
-            sxx, syy, szz = at(SXX), at(SYY), at(SZZ)
-            ux, uy, uz = u(0), u(1), u(2)
-            fxx = ux - u(0, -1)
-            fyy = uy - u(1, 0, -1)
-            fzz = zminus(uz)
-            lam = (fxx + fyy + fzz) * (sxx + syy + szz)
-            mu = (
-                2.0 * (fxx * sxx + fyy * syy + fzz * szz)
-                + ((u(1, 1) - uy) + (u(0, 0, 1) - ux)) * at(SXY)
-                + ((u(2, 1) - uz) + zplus(ux)) * at(SXZ)
-                + ((u(2, 0, 1) - uz) + zplus(uy)) * at(SYZ)
-            )
-            rho = at(VX) * (w(0) - ux) + at(VY) * (w(1) - uy) + at(VZ) * (w(2) - uz)
-            for ref, term in zip(G, (lam, mu, rho)):
-                ref[x - 1, flat, :] = term if step == 0 else ref[x - 1, flat, :] + term
+            add_terms(step, x, y, *[F[k][x, pl.ds(PAD + y, ROWS), :] for k in range(9)])
         return carry
 
     def densify():
@@ -444,17 +451,22 @@
     wait_recv(forward_halo())
     lax.fori_loop(0, 4, later_products, 0)
 
-    lax.fori_loop(2, CX, speeds, 0)
+    def planes(first, stop, body):
+        lax.fori_loop(first, stop, body, 0)
+
+    both = [functools.partial(stresses, t, add=True) for t in range(STEPS)]
     wait_recv(edge_halo(1))
-    end_planes(1)
-    stresses(1, 1)
-    stresses(1, CX)
+    edges_in(1)
+    for x in (1, 2, CX - 1, CX):
+        speeds(x)
+    both[1](1)
+    both[1](CX)
     edges_out(2)
     start(edge_halo(2))
-    lax.fori_loop(2, CX, functools.partial(stresses, 1), 0)
-    lax.fori_loop(1, CX + 1, functools.partial(gradients, 1), 0)
-
-    lax.fori_loop(2, CX, speeds, 0)
+    planes(3, CX - 1, speeds)
+    low, high = 2 * GROUPS[0][0] + 1, 2 * (GROUPS[0][0] + GROUPS[0][1]) + 1
+    planes(low - 2, high + 2, both[1])
+    planes(low - 1, high + 1, speeds)
 
     def to_mate(n):
         pairs = pl.ds(*GROUPS[n])
@@ -505,20 +517,22 @@
         pairs_of(n, sum_cross)
         to_cross(n).start()
 
-    def last(x, carry):
-        stresses(STEPS - 1, x)
-        gradients(STEPS - 1, x)
-        return carry
-
     for n, (first, count) in enumerate(GROUPS):
-        if n == 1:
-            wait_recv(edge_halo(2))
-            end_planes(2)
-        lax.fori_loop(2 * first + 1, 2 * (first + count) + 1, last, 0)
+        planes(2 * first + 1, 2 * (first + count) + 1, both[2])
         pairs_of(n, slabs)
         for c in to_mate(n):
             c.start()
-        if n > 0:
+        if n == 0:
+            planes(2, low - 2, both[1])
+            planes(high + 2, CX, both[1])
+            pass_on(0)
+            planes(2, low - 1, speeds)
+            planes(high + 1, CX, speeds)
+            wait_recv(edge_halo(2))
+            edges_in(2)
+            speeds(1)
+            speeds(CX)
+        elif n > 1:
             pass_on(n - 1)
     pass_on(len(GROUPS) - 1)
 

time: 57.7 us -> 55.3 us (0.958)
  Pallas kernels: 57 us -> 54.5 us
    pallas_call x1, Pallas kernels: 53.1 us -> 50.7 us  [local(): pl.pallas_call(kernel, out_shape=tuple((pltpu.VMEM(shape, F32) for shape...]
where the time goes in v4:
time: 55.3 us; the launch traced here: 55.2 us
  Pallas kernels  54.5 us (99%)
  between operations  0.64 us (1%)
    pallas_call x1, Pallas kernels, local(): pl.pallas_call(kernel, out_shape=tuple((pltpu.VMEM(shape, F32) for shape...  50.7 us
    pallas_call x1, Pallas kernels, local(): pl.pallas_call(finish, out_shape=(jax.ShapeDtypeStruct((1, 9, CX, NY, NZ)...  3.88 us

profile of v4, /device:TPU:9, one launch (start us, length us, event | category | flops | bytes accessed | tf_op | source)
XLA Modules:
  0.0 55.2 jit_solution(12563601835583847991)
XLA Ops:
  0.6 50.7 %shard_map.95 = (f32[18,80,128]{2,1,0:T(8,128)S(1)}, f32[18,80,128]{2,1,0:T(8,128)S(1)}, f32[18,80,128]{2,1,0:T(8,128)S(1)}, f32[18,80,128]{2,1,0:T(8,128)S(1)},...) custom-call(f32[1,9,16,64,128]{4,3,2,1,0:T(8,128)} %adj.1, ...), custom_call_target="tpu_custom_call" | custom-call | tf_op jit(solution)/shard_map/pallas_call | solution.py:656
  51.3 3.9 %shard_map.96 = (f32[1,9,16,64,128]{4,3,2,1,0:T(8,128)}, f32[3,16,16,128]{3,2,1,0:T(8,128)}) custom-call(f32[18,80,128]{2,1,0:T(8,128)S(1)} %get-tuple-element.12.f0, f32[18,80,128]{2,1,0:T(8,128)S(1)} %get-tuple-element.13.f1, f32[18,80,128]{2,1,0:T(8,128)S(1)} %get-tuple-element.14.f2, f32[18,80,128]{2,1,0:T(8,128)S(1)} %get-tuple-element.15.f3, ...), custom_call_target="tpu_custom_call" | custom-call | tf_op jit(solution)/shard_map/pallas_call | solution.py:665

commit v5 on v4

--- a/solution.py
+++ b/solution.py
@@ -41,13 +41,24 @@
     return jnp.where(lane_of(f.shape[0]) == NZ - 1, 0.0, rolled) - f
 
 
+def near(h, k, p, lo, n):
+    def at(dp=0, dy=0):
+        return h[k, p + dp, pl.ds(lo + dy, n), :]
+
+    mid = at()
+    lane = lane_of(n)
+    total = at(1) + at(-1) + at(0, 1) + at(0, -1)
+    total = total + jnp.where(lane == NZ - 1, 0.0, pltpu.roll(mid, NZ - 1, 1)) + jnp.where(lane == 0, 0.0, pltpu.roll(mid, 1, 1))
+    return mid + KAPPA * (total - 6.0 * mid)
+
+
 def kernel(
     adj, fwd, vp_h, sr_h, dn_h, res_h, own_h, cell_h,
-    f0, f1, f2, f3, f4, f5, f6, f7, f8, h0,
+    f0, f1, f2, f3, f4, f5, f6, f7, f8, h1,
     fw, dense, cb, cl, cm, g0, g1, g2,
     to_left, to_right, from_left, from_right, edge_b, rho_end,
     res, own, cell, packed, arrived, a_one, b_one,
-    gs, rb1, s2, rb2,
+    gs, rb1, s2, rb2, h0,
     load_f, load_w, load_p, load_e, load_c,
     halo_s, halo_r, eb_s, eb_r, fh_s, fh_r, a2a_s, a2a_r,
     r1_s, r1_r, r2_s, r2_r, gx_s, gx_r,
@@ -375,6 +386,19 @@
             add_terms(step, x, y, *[F[k][x, pl.ds(PAD + y, ROWS), :] for k in range(9)])
         return carry
 
+    def tile(v):
+        return jnp.broadcast_to(v, (16, CAP)).astype(BF16)
+
+    def values(s, steps):
+        row = arrived[s]
+        zone = (row[5:6].astype(I32) == lax.broadcasted_iota(I32, (NZ, CAP), 0)).astype(F32).astype(BF16)
+        zone = zone.reshape(NZ // 16, 16, CAP)
+        for t in steps:
+            v = row[t : t + 1]
+            hi = v.astype(BF16).astype(F32)
+            b_one[t, s, pl.ds(0, NZ), :] = (zone * tile(hi)[None]).reshape(NZ, CAP)
+            b_one[t, s, pl.ds(NZ, NZ), :] = (zone * tile(v - hi)[None]).reshape(NZ, CAP)
+
     def densify():
         def channel_wait(k, carry):
             channel_copy(k).wait_recv()
@@ -384,22 +408,13 @@
 
         def one_hot(s, carry):
             row = arrived[s]
-            x, y, z = row[3:4].astype(I32), row[4:5].astype(I32), row[5:6].astype(I32)
-
-            def tile(v):
-                return jnp.broadcast_to(v, (16, CAP)).astype(BF16)
-
+            x, y = row[3:4].astype(I32), row[4:5].astype(I32)
             yone = (y == lax.broadcasted_iota(I32, (NY, CAP), 0)).astype(F32).astype(BF16)
-            zone = (z == lax.broadcasted_iota(I32, (NZ, CAP), 0)).astype(F32).astype(BF16)
-            yone, zone = yone.reshape(NY // 16, 16, CAP), zone.reshape(NZ // 16, 16, CAP)
+            yone = yone.reshape(NY // 16, 16, CAP)
             for i in range(CX):
                 xone = tile((x == i).astype(F32))
                 a_one[s, pl.ds(i * NY, NY), :] = (yone * xone[None]).reshape(NY, CAP)
-            for t in range(STEPS):
-                v = row[t : t + 1]
-                hi = v.astype(BF16).astype(F32)
-                b_one[t, s, pl.ds(0, NZ), :] = (zone * tile(hi)[None]).reshape(NZ, CAP)
-                b_one[t, s, pl.ds(NZ, NZ), :] = (zone * tile(v - hi)[None]).reshape(NZ, CAP)
+            values(s, (0,))
             return carry
 
         lax.fori_loop(0, N_SPACE, one_hot, 0)
@@ -413,6 +428,8 @@
         dense[t, pl.ds(4 * m, 4), :, :] = (got[:, :NZ] + got[:, NZ:]).reshape(4, NY, NZ)
 
     def first_product(m, carry):
+        for i in range(N_SPACE // 4):
+            values(N_SPACE // 4 * m + i, (1, 2))
         product(m, 0)
         for i in range(4):
             x = 4 * m + i + 1
@@ -424,6 +441,8 @@
             product(m, t)
         for i in range(4):
             gradients(0, 4 * m + i + 1)
+        for i in range(3):
+            speeds(3 * m + i + 2)
         return carry
 
     def end_planes(step):
@@ -457,13 +476,12 @@
     both = [functools.partial(stresses, t, add=True) for t in range(STEPS)]
     wait_recv(edge_halo(1))
     edges_in(1)
-    for x in (1, 2, CX - 1, CX):
+    for x in (1, CX - 2, CX - 1, CX):
         speeds(x)
     both[1](1)
     both[1](CX)
     edges_out(2)
     start(edge_halo(2))
-    planes(3, CX - 1, speeds)
     low, high = 2 * GROUPS[0][0] + 1, 2 * (GROUPS[0][0] + GROUPS[0][1]) + 1
     planes(low - 2, high + 2, both[1])
     planes(low - 1, high + 1, speeds)
@@ -549,12 +567,26 @@
         [send(h0.at[:, pl.ds(2, 2), rim], h0.at[:, pl.ds(CX + 2, 2), rim], gx_s.at[0], gx_r.at[0], left)],
         [send(h0.at[:, pl.ds(CX, 2), rim], h0.at[:, pl.ds(0, 2), rim], gx_s.at[1], gx_r.at[1], right)],
     )
+    def sweep_one(p, carry):
+        gx = CX * me + p - 2
+        gy = 16 * sh - 2 + lax.broadcasted_iota(I32, (24, NZ), 0)
+        keep = (gy >= 0) & (gy < NY) & (gx >= 0) & (gx < NX)
+        for k in range(3):
+            h1[k, p, rim, :] = jnp.where(keep, near(h0, k, p, 8, 24), 0.0)
+        return carry
+
     for n in range(len(GROUPS)):
         to_cross(n).wait_recv()
         pairs_of(n, sum_own)
         if n == 2:
             start(grad_halo)
+        if n == 3:
+            planes(3, 11, sweep_one)
+        if n == 4:
+            planes(11, CX + 1, sweep_one)
     wait_recv(grad_halo)
+    planes(1, 3, sweep_one)
+    planes(CX + 1, CX + 3, sweep_one)
     wait_send(grad_halo)
 
     for step in range(STEPS):
@@ -573,43 +605,26 @@
         to_cross(n).wait_send()
 
 
-def finish(f0, f1, f2, f3, f4, f5, f6, f7, f8, h0, out_adj, out_grad, h1, og, sem):
-    me = lax.axis_index("space")
-    sh = lax.axis_index("shot")
+def finish(f0, f1, f2, f3, f4, f5, f6, f7, f8, h1, out_adj, out_grad, og, sem):
     fields = (f0, f1, f2, f3, f4, f5, f6, f7, f8)
     stores = [pltpu.make_async_copy(f.at[pl.ds(1, CX), pl.ds(PAD, NY)], out_adj.at[0, k], sem.at[k]) for k, f in enumerate(fields)]
     for c in stores:
         c.start()
 
-    def near(h, k, p, lo, n):
-        def at(dp=0, dy=0):
-            return h[k, p + dp, pl.ds(lo + dy, n), :]
-
-        mid = at()
-        lane = lane_of(n)
-        total = at(1) + at(-1) + at(0, 1) + at(0, -1)
-        total = total + jnp.where(lane == NZ - 1, 0.0, pltpu.roll(mid, NZ - 1, 1)) + jnp.where(lane == 0, 0.0, pltpu.roll(mid, 1, 1))
-        return mid + KAPPA * (total - 6.0 * mid)
-
-    def sweep_one(p, carry):
-        gx = CX * me + p - 2
-        gy = 16 * sh - 2 + lax.broadcasted_iota(I32, (24, NZ), 0)
-        keep = (gy >= 0) & (gy < NY) & (gx >= 0) & (gx < NX)
-        for k in range(3):
-            h1[k, p, pl.ds(8, 24), :] = jnp.where(keep, near(h0, k, p, 8, 24), 0.0)
-        return carry
-
-    lax.fori_loop(1, CX + 3, sweep_one, 0)
-
     def sweep_two(x, carry):
         for k in range(3):
             og[k, x] = near(h1, k, x + 2, 10, 16)
         return carry
 
-    lax.fori_loop(0, CX, sweep_two, 0)
-    grad_out = pltpu.make_async_copy(og, out_grad, sem.at[9])
-    grad_out.start()
-    grad_out.wait()
+    half = CX // 2
+    parts = []
+    for i in range(2):
+        lax.fori_loop(half * i, half * (i + 1), sweep_two, 0)
+        part = pl.ds(half * i, half)
+        parts.append(pltpu.make_async_copy(og.at[:, part], out_grad.at[:, part], sem.at[9 + i]))
+        parts[i].start()
+    for c in parts:
+        c.wait()
     for c in stores:
         c.wait()
 
@@ -645,6 +660,7 @@
             pltpu.VMEM((2, 3, CX // 2, 40, NZ), F32),
             pltpu.VMEM((3, CX // 2, 40, NZ), F32),
             pltpu.VMEM((3, CX // 2, 40, NZ), F32),
+            pltpu.VMEM((3, CX + 4, 40, NZ), F32),
         ]
         + [dma((9,)), dma((4,)), dma((3,)), dma((10, 2)), dma((3,))]
         + [dma((STEPS, 2)), dma((STEPS, 2)), dma((2,)), dma((2,)), dma((2,)), dma((2,)), dma((N_SPACE,)), dma((N_SPACE,))]
@@ -670,7 +686,7 @@
         ),
         in_specs=[vmem] * len(held),
         out_specs=(hbm, hbm),
-        scratch_shapes=[pltpu.VMEM((3, CX + 4, 40, NZ), F32), pltpu.VMEM((3, CX, 16, NZ), F32), dma((10,))],
+        scratch_shapes=[pltpu.VMEM((3, CX, 16, NZ), F32), dma((11,))],
         compiler_params=pltpu.CompilerParams(vmem_limit_bytes=8 * 1024 * 1024),
     )(*kept)
 

time: 55.3 us -> 54.3 us (0.982)
  Pallas kernels: 54.5 us -> 53.6 us
    pallas_call x1, Pallas kernels: 3.88 us -> 2.39 us  [local(): pl.pallas_call(finish, out_shape=(jax.ShapeDtypeStruct((1, 9, CX, NY, NZ)...]
where the time goes in v5:
time: 54.3 us; the launch traced here: 54.2 us
  Pallas kernels  53.6 us (99%)
  between operations  0.64 us (1%)
    pallas_call x1, Pallas kernels, local(): pl.pallas_call(kernel, out_shape=tuple((pltpu.VMEM(shape, F32) for shape...  51.2 us
    pallas_call x1, Pallas kernels, local(): pl.pallas_call(finish, out_shape=(jax.ShapeDtypeStruct((1, 9, CX, NY, NZ)...  2.39 us

profile of v5, /device:TPU:9, one launch (start us, length us, event | category | flops | bytes accessed | tf_op | source)
XLA Modules:
  0.0 54.2 jit_solution(3955924700897887997)
XLA Ops:
  0.6 51.2 %shard_map.95 = (f32[18,80,128]{2,1,0:T(8,128)S(1)}, f32[18,80,128]{2,1,0:T(8,128)S(1)}, f32[18,80,128]{2,1,0:T(8,128)S(1)}, f32[18,80,128]{2,1,0:T(8,128)S(1)},...) custom-call(f32[1,9,16,64,128]{4,3,2,1,0:T(8,128)} %adj.1, ...), custom_call_target="tpu_custom_call" | custom-call | tf_op jit(solution)/shard_map/pallas_call | solution.py:672
  51.8 2.4 %shard_map.96 = (f32[1,9,16,64,128]{4,3,2,1,0:T(8,128)}, f32[3,16,16,128]{3,2,1,0:T(8,128)}) custom-call(f32[18,80,128]{2,1,0:T(8,128)S(1)} %get-tuple-element.12.f0, f32[18,80,128]{2,1,0:T(8,128)S(1)} %get-tuple-element.13.f1, f32[18,80,128]{2,1,0:T(8,128)S(1)} %get-tuple-element.14.f2, f32[18,80,128]{2,1,0:T(8,128)S(1)} %get-tuple-element.15.f3, ...), custom_call_target="tpu_custom_call" | custom-call | tf_op jit(solution)/shard_map/pallas_call | solution.py:681

commit v6 on v5

--- a/solution.py
+++ b/solution.py
@@ -476,12 +476,15 @@
     both = [functools.partial(stresses, t, add=True) for t in range(STEPS)]
     wait_recv(edge_halo(1))
     edges_in(1)
-    for x in (1, CX - 2, CX - 1, CX):
+    for x in (1, CX - 1, CX):
         speeds(x)
-    both[1](1)
-    both[1](CX)
+    stresses(1, 1)
+    stresses(1, CX)
     edges_out(2)
     start(edge_halo(2))
+    speeds(CX - 2)
+    gradients(1, 1)
+    gradients(1, CX)
     low, high = 2 * GROUPS[0][0] + 1, 2 * (GROUPS[0][0] + GROUPS[0][1]) + 1
     planes(low - 2, high + 2, both[1])
     planes(low - 1, high + 1, speeds)

time: 54.3 us -> 54.2 us (level)
  no operation moved by 1% of the time
where the time goes in v6:
time: 54.2 us; the launch traced here: 54.1 us
  Pallas kernels  53.5 us (99%)
  between operations  0.64 us (1%)
    pallas_call x1, Pallas kernels, local(): pl.pallas_call(kernel, out_shape=tuple((pltpu.VMEM(shape, F32) for shape...  51.1 us
    pallas_call x1, Pallas kernels, local(): pl.pallas_call(finish, out_shape=(jax.ShapeDtypeStruct((1, 9, CX, NY, NZ)...  2.39 us

profile of v6, /device:TPU:9, one launch (start us, length us, event | category | flops | bytes accessed | tf_op | source)
XLA Modules:
  0.0 54.1 jit_solution(11098607220958941189)
XLA Ops:
  0.6 51.1 %shard_map.95 = (f32[18,80,128]{2,1,0:T(8,128)S(1)}, f32[18,80,128]{2,1,0:T(8,128)S(1)}, f32[18,80,128]{2,1,0:T(8,128)S(1)}, f32[18,80,128]{2,1,0:T(8,128)S(1)},...) custom-call(f32[1,9,16,64,128]{4,3,2,1,0:T(8,128)} %adj.1, ...), custom_call_target="tpu_custom_call" | custom-call | tf_op jit(solution)/shard_map/pallas_call | solution.py:675
  51.7 2.4 %shard_map.96 = (f32[1,9,16,64,128]{4,3,2,1,0:T(8,128)}, f32[3,16,16,128]{3,2,1,0:T(8,128)}) custom-call(f32[18,80,128]{2,1,0:T(8,128)S(1)} %get-tuple-element.12.f0, f32[18,80,128]{2,1,0:T(8,128)S(1)} %get-tuple-element.13.f1, f32[18,80,128]{2,1,0:T(8,128)S(1)} %get-tuple-element.14.f2, f32[18,80,128]{2,1,0:T(8,128)S(1)} %get-tuple-element.15.f3, ...), custom_call_target="tpu_custom_call" | custom-call | tf_op jit(solution)/shard_map/pallas_call | solution.py:684
